TPU v7x, 256 devices: a whole 4x4x8 slice. The times are simulated.
256 devices in a mesh: blk: 8 (over z), uly: 32 (over x, y, core).
Axes of the slice: x: 4, y: 4, z: 8, core: 2. Of those that a mesh axis runs over, the one named last changes fastest.
Arguments:
- queries: bfloat16 [16384, 4096], P(('blk', 'uly')), may hold values from -120 to 120
- keys: bfloat16 [16384, 4096], P(('blk', 'uly')), may hold values from -30 to 30
- values: bfloat16 [16384, 4096], P(('blk', 'uly')), may hold values from -6 to 6
Outputs:
- attended: bfloat16 [16384, 4096], P(('blk', 'uly'))
- key_cache: bfloat16 [16384, 4096], P(('blk', 'uly'))
All inputs are finite; a program needn't handle non-finite values.
Results may differ from a plain program's by a relative error of at most 0.0069.
Values may be sent and summed in bfloat16 or wider, within the bound.
No kernel may reach another device: no remote copies, remote signals or barrier semaphores. Data moves between devices by JAX's collectives and lax.ppermute only.
A program may use at most 64 MiB of HBM per device.

v0:
```python
import math

import jax
import jax.numpy as jnp
from jax import lax
from jax.sharding import PartitionSpec as P

HD = 128


def shards(queries, keys, values):
    tok_rows = queries.shape[0]
    cycle = lax.axis_size("blk")
    inner = lax.axis_size("uly")
    total_rows = tok_rows * cycle * inner
    keys32 = keys.astype(jnp.float32)
    key_mean = lax.psum(jnp.sum(keys32, axis=0), ("blk", "uly")) / total_rows
    key_cache = (keys32 - key_mean).astype(jnp.bfloat16)
    stacked = jnp.stack([queries, key_cache, values])
    grouped = lax.all_to_all(stacked, "uly", split_axis=2, concat_axis=1, tiled=True)
    group_rows = tok_rows * inner
    heads_here = grouped.shape[2] // HD
    split_heads = grouped.reshape(3, group_rows, heads_here, HD).transpose(0, 2, 1, 3)
    mine = lax.axis_index("blk")
    local_q = split_heads[0].reshape(heads_here, 1, group_rows, HD)
    pieces = 1
    starts = jnp.reshape(mine * group_rows, (1,))
    scale = 1.0 / math.sqrt(HD)
    kv_pair = split_heads[1:]
    initial = (
        jnp.full((heads_here, pieces, group_rows), -1e30, jnp.float32),
        jnp.zeros((heads_here, pieces, group_rows), jnp.float32),
        jnp.zeros((heads_here, pieces, group_rows, HD), jnp.float32),
    )

    def make_update(index, k_block, v_block, k_pos):
        q_piece = local_q[:, index]
        q_pos = starts[index] + jnp.arange(group_rows, dtype=jnp.int32)

        def update(state):
            run_max, run_sum, accum = state
            scores = (
                jnp.einsum("hqd,hkd->hqk", q_piece, k_block, preferred_element_type=jnp.float32)
                * scale
            )
            mask = (k_pos[None, :] <= q_pos[:, None])[None]
            old_max = run_max[:, index]
            new_max = jnp.maximum(old_max, jnp.max(jnp.where(mask, scores, -1e30), axis=2))
            weights = jnp.where(mask, jnp.exp(scores - new_max[:, :, None]), 0.0)
            factor = jnp.exp(old_max - new_max)
            new_sum = run_sum[:, index] * factor + jnp.sum(weights, axis=2)
            added = jnp.einsum(
                "hqk,hkd->hqd",
                weights.astype(jnp.bfloat16),
                v_block,
                preferred_element_type=jnp.float32,
            )
            new_acc = accum[:, index] * factor[:, :, None] + added
            return (
                run_max.at[:, index].set(new_max),
                run_sum.at[:, index].set(new_sum),
                accum.at[:, index].set(new_acc),
            )

        return update

    def keep_state(state):
        return state

    piece = lax.all_gather(kv_pair, "blk", axis=2, tiled=True)
    rows = piece.shape[2]
    sub_rows = math.gcd(rows, 512)

    def step(turn, state):
        k_block = lax.dynamic_slice_in_dim(piece[0], turn * sub_rows, sub_rows, 1)
        v_block = lax.dynamic_slice_in_dim(piece[1], turn * sub_rows, sub_rows, 1)
        k_start = turn * sub_rows
        k_pos = k_start + jnp.arange(sub_rows, dtype=jnp.int32)
        needed = k_start <= starts[0] + group_rows - 1
        state = lax.cond(needed, make_update(0, k_block, v_block, k_pos), keep_state, state)
        return state

    run_max, run_sum, accum = lax.fori_loop(0, rows // sub_rows, step, initial)
    result = (accum / run_sum[..., None]).astype(jnp.bfloat16)
    merged = (
        result.reshape(heads_here, group_rows, HD)
        .transpose(1, 0, 2)
        .reshape(group_rows, heads_here * HD)
    )
    attended = lax.all_to_all(merged, "uly", split_axis=0, concat_axis=1, tiled=True)
    return (attended, key_cache)


def solution(mesh):
    in_specs = (P(("blk", "uly"), None), P(("blk", "uly"), None), P(("blk", "uly"), None))
    out_specs = (P(("blk", "uly"), None), P(("blk", "uly"), None))
    return jax.shard_map(shards, mesh=mesh, in_specs=in_specs, out_specs=out_specs, check_vma=False)
```

profile of v0, /device:TPU:225, one launch (start us, length us, event | category | flops | bytes accessed | tf_op | source)
XLA Modules:
  0.0 487.2 jit_solution(10372374282996666961)
XLA Ops:
  8.4 75.8 %psum.7 = f32[4096]{0:T(1024)S(1)} all-reduce(f32[4096]{0:T(1024)S(1)} %convert_reduce_fusion), channel_id=1, replica_groups=mesh['blk'=8,'uly'=32] {'blk','uly'}, use_global_device_ids=true, to_apply=%region_1.0 | all-reduce | flops 4096 | bytes 32768 | tf_op jit(solution)/shard_map/psum | solution.py:17
  86.7 4.8 copy.14
  91.4 6.1 %reshape.245 = bf16[32,2,12288]{2,1,0:T(2,128)(2,1)S(1)} reshape(bf16[4096,3,64]{2,1,0:T(4,128)(2,1)} %bitcast.55) | data formatting | bytes 3145728
  97.5 26.7 %all_to_all.34 = bf16[32,2,12288]{2,1,0:T(2,128)(2,1)S(1)} all-to-all(bf16[32,2,12288]{2,1,0:T(2,128)(2,1)S(1)} %reshape.245), channel_id=1, replica_groups=mesh['blk'=8,'uly'=32] {'uly'}, dimensions={0} | all-to-all | bytes 3145728 | tf_op jit(solution)/shard_map/all_to_all | solution.py:20
  124.3 4.8 reshape.246
  129.1 4.7 slice.102
  133.8 3.9 copy.15
  137.7 3.9 slice.103
  143.9 83.1 %all-gather.2.cloned.1.call-done = bf16[2,1,16384,128]{3,2,1,0:T(8,128)(2,1)} async-done(((bf16[2,1,2048,128]{3,2,1,0:T(8,128)(2,1)}), bf16[2,1,16384,128]{3,2,1,0:T(8,128)(2,1)}) %all-gather.2.cloned.1.call-update) | async-done | bytes 8388624 | tf_op jit(solution)/shard_map/all_gather | solution.py:70
  227.2 231.9 %while.22 = (s32[]{:T(128)}, f32[1,1,2048]{2,1,0:T(1,128)S(1)}, f32[1,1,2048]{2,1,0:T(1,128)S(1)}, f32[1,1,2048,128]{3,2,1,0:T(8,128)S(1)}, s32[]{:T(128)}, /*in...) while((s32[]{:T(128)}, f32[1,1,2048]{2,1,0:T(1,128)S(1)}, ...), condition=%wide.region_7.8_spmd, body=%wide.region_2.7_spmd.sunk | while | flops 552086016 | bytes 32428336 | solution.py:83
  227.2 7.2 %conditional.2 = ((f32[1,1,2048]{2,1,0:T(1,128)S(1)}, f32[1,1,2048]{2,1,0:T(1,128)S(1)}, f32[1,1,2048,128]{3,2,1,0:T(8,128)S(1)})) conditional(s32[]{:T(128)} %convert_element_type.41, (f32[1,1,2048]{2,1,0:T(1,128)S(1)}, f32[1,1,2048]{2,1,0:T(1,128)S(1)}, f32[1,1,2048,128]{3,2,1,0:T(8,128)S(1)}) %tuple.75, (s32[]{:T(128)}, s32[512]{0:T(512)S(1)}, ...), branch_computations={%region_3.0_spmd, %region_4.6_spmd} | conditional | flops 552086016 | bytes 32417872 | solution.py:80
  227.3 3.8 fusion.21
  234.5 7.2 %conditional.2 = ((f32[1,1,2048]{2,1,0:T(1,128)S(1)}, f32[1,1,2048]{2,1,0:T(1,128)S(1)}, f32[1,1,2048,128]{3,2,1,0:T(8,128)S(1)})) conditional(s32[]{:T(128)} %convert_element_type.41, (f32[1,1,2048]{2,1,0:T(1,128)S(1)}, f32[1,1,2048]{2,1,0:T(1,128)S(1)}, f32[1,1,2048,128]{3,2,1,0:T(8,128)S(1)}) %tuple.75, (s32[]{:T(128)}, s32[512]{0:T(512)S(1)}, ...), branch_computations={%region_3.0_spmd, %region_4.6_spmd} | conditional | flops 552086016 | bytes 32417872 | solution.py:80
  241.8 7.2 %conditional.2 = ((f32[1,1,2048]{2,1,0:T(1,128)S(1)}, f32[1,1,2048]{2,1,0:T(1,128)S(1)}, f32[1,1,2048,128]{3,2,1,0:T(8,128)S(1)})) conditional(s32[]{:T(128)} %convert_element_type.41, (f32[1,1,2048]{2,1,0:T(1,128)S(1)}, f32[1,1,2048]{2,1,0:T(1,128)S(1)}, f32[1,1,2048,128]{3,2,1,0:T(8,128)S(1)}) %tuple.75, (s32[]{:T(128)}, s32[512]{0:T(512)S(1)}, ...), branch_computations={%region_3.0_spmd, %region_4.6_spmd} | conditional | flops 552086016 | bytes 32417872 | solution.py:80
  241.8 3.8 fusion.21
  249.0 7.2 %conditional.2 = ((f32[1,1,2048]{2,1,0:T(1,128)S(1)}, f32[1,1,2048]{2,1,0:T(1,128)S(1)}, f32[1,1,2048,128]{3,2,1,0:T(8,128)S(1)})) conditional(s32[]{:T(128)} %convert_element_type.41, (f32[1,1,2048]{2,1,0:T(1,128)S(1)}, f32[1,1,2048]{2,1,0:T(1,128)S(1)}, f32[1,1,2048,128]{3,2,1,0:T(8,128)S(1)}) %tuple.75, (s32[]{:T(128)}, s32[512]{0:T(512)S(1)}, ...), branch_computations={%region_3.0_spmd, %region_4.6_spmd} | conditional | flops 552086016 | bytes 32417872 | solution.py:80
  256.2 7.2 %conditional.2 = ((f32[1,1,2048]{2,1,0:T(1,128)S(1)}, f32[1,1,2048]{2,1,0:T(1,128)S(1)}, f32[1,1,2048,128]{3,2,1,0:T(8,128)S(1)})) conditional(s32[]{:T(128)} %convert_element_type.41, (f32[1,1,2048]{2,1,0:T(1,128)S(1)}, f32[1,1,2048]{2,1,0:T(1,128)S(1)}, f32[1,1,2048,128]{3,2,1,0:T(8,128)S(1)}) %tuple.75, (s32[]{:T(128)}, s32[512]{0:T(512)S(1)}, ...), branch_computations={%region_3.0_spmd, %region_4.6_spmd} | conditional | flops 552086016 | bytes 32417872 | solution.py:80
  263.5 7.2 %conditional.2 = ((f32[1,1,2048]{2,1,0:T(1,128)S(1)}, f32[1,1,2048]{2,1,0:T(1,128)S(1)}, f32[1,1,2048,128]{3,2,1,0:T(8,128)S(1)})) conditional(s32[]{:T(128)} %convert_element_type.41, (f32[1,1,2048]{2,1,0:T(1,128)S(1)}, f32[1,1,2048]{2,1,0:T(1,128)S(1)}, f32[1,1,2048,128]{3,2,1,0:T(8,128)S(1)}) %tuple.75, (s32[]{:T(128)}, s32[512]{0:T(512)S(1)}, ...), branch_computations={%region_3.0_spmd, %region_4.6_spmd} | conditional | flops 552086016 | bytes 32417872 | solution.py:80
  270.7 7.2 %conditional.2 = ((f32[1,1,2048]{2,1,0:T(1,128)S(1)}, f32[1,1,2048]{2,1,0:T(1,128)S(1)}, f32[1,1,2048,128]{3,2,1,0:T(8,128)S(1)})) conditional(s32[]{:T(128)} %convert_element_type.41, (f32[1,1,2048]{2,1,0:T(1,128)S(1)}, f32[1,1,2048]{2,1,0:T(1,128)S(1)}, f32[1,1,2048,128]{3,2,1,0:T(8,128)S(1)}) %tuple.75, (s32[]{:T(128)}, s32[512]{0:T(512)S(1)}, ...), branch_computations={%region_3.0_spmd, %region_4.6_spmd} | conditional | flops 552086016 | bytes 32417872 | solution.py:80
  270.8 3.8 fusion.21
  278.0 7.2 %conditional.2 = ((f32[1,1,2048]{2,1,0:T(1,128)S(1)}, f32[1,1,2048]{2,1,0:T(1,128)S(1)}, f32[1,1,2048,128]{3,2,1,0:T(8,128)S(1)})) conditional(s32[]{:T(128)} %convert_element_type.41, (f32[1,1,2048]{2,1,0:T(1,128)S(1)}, f32[1,1,2048]{2,1,0:T(1,128)S(1)}, f32[1,1,2048,128]{3,2,1,0:T(8,128)S(1)}) %tuple.75, (s32[]{:T(128)}, s32[512]{0:T(512)S(1)}, ...), branch_computations={%region_3.0_spmd, %region_4.6_spmd} | conditional | flops 552086016 | bytes 32417872 | solution.py:80
  278.0 3.8 fusion.21
  285.2 7.2 %conditional.2 = ((f32[1,1,2048]{2,1,0:T(1,128)S(1)}, f32[1,1,2048]{2,1,0:T(1,128)S(1)}, f32[1,1,2048,128]{3,2,1,0:T(8,128)S(1)})) conditional(s32[]{:T(128)} %convert_element_type.41, (f32[1,1,2048]{2,1,0:T(1,128)S(1)}, f32[1,1,2048]{2,1,0:T(1,128)S(1)}, f32[1,1,2048,128]{3,2,1,0:T(8,128)S(1)}) %tuple.75, (s32[]{:T(128)}, s32[512]{0:T(512)S(1)}, ...), branch_computations={%region_3.0_spmd, %region_4.6_spmd} | conditional | flops 552086016 | bytes 32417872 | solution.py:80
  292.5 7.2 %conditional.2 = ((f32[1,1,2048]{2,1,0:T(1,128)S(1)}, f32[1,1,2048]{2,1,0:T(1,128)S(1)}, f32[1,1,2048,128]{3,2,1,0:T(8,128)S(1)})) conditional(s32[]{:T(128)} %convert_element_type.41, (f32[1,1,2048]{2,1,0:T(1,128)S(1)}, f32[1,1,2048]{2,1,0:T(1,128)S(1)}, f32[1,1,2048,128]{3,2,1,0:T(8,128)S(1)}) %tuple.75, (s32[]{:T(128)}, s32[512]{0:T(512)S(1)}, ...), branch_computations={%region_3.0_spmd, %region_4.6_spmd} | conditional | flops 552086016 | bytes 32417872 | solution.py:80
  299.7 7.2 %conditional.2 = ((f32[1,1,2048]{2,1,0:T(1,128)S(1)}, f32[1,1,2048]{2,1,0:T(1,128)S(1)}, f32[1,1,2048,128]{3,2,1,0:T(8,128)S(1)})) conditional(s32[]{:T(128)} %convert_element_type.41, (f32[1,1,2048]{2,1,0:T(1,128)S(1)}, f32[1,1,2048]{2,1,0:T(1,128)S(1)}, f32[1,1,2048,128]{3,2,1,0:T(8,128)S(1)}) %tuple.75, (s32[]{:T(128)}, s32[512]{0:T(512)S(1)}, ...), branch_computations={%region_3.0_spmd, %region_4.6_spmd} | conditional | flops 552086016 | bytes 32417872 | solution.py:80
  307.0 7.2 %conditional.2 = ((f32[1,1,2048]{2,1,0:T(1,128)S(1)}, f32[1,1,2048]{2,1,0:T(1,128)S(1)}, f32[1,1,2048,128]{3,2,1,0:T(8,128)S(1)})) conditional(s32[]{:T(128)} %convert_element_type.41, (f32[1,1,2048]{2,1,0:T(1,128)S(1)}, f32[1,1,2048]{2,1,0:T(1,128)S(1)}, f32[1,1,2048,128]{3,2,1,0:T(8,128)S(1)}) %tuple.75, (s32[]{:T(128)}, s32[512]{0:T(512)S(1)}, ...), branch_computations={%region_3.0_spmd, %region_4.6_spmd} | conditional | flops 552086016 | bytes 32417872 | solution.py:80
  314.2 7.2 %conditional.2 = ((f32[1,1,2048]{2,1,0:T(1,128)S(1)}, f32[1,1,2048]{2,1,0:T(1,128)S(1)}, f32[1,1,2048,128]{3,2,1,0:T(8,128)S(1)})) conditional(s32[]{:T(128)} %convert_element_type.41, (f32[1,1,2048]{2,1,0:T(1,128)S(1)}, f32[1,1,2048]{2,1,0:T(1,128)S(1)}, f32[1,1,2048,128]{3,2,1,0:T(8,128)S(1)}) %tuple.75, (s32[]{:T(128)}, s32[512]{0:T(512)S(1)}, ...), branch_computations={%region_3.0_spmd, %region_4.6_spmd} | conditional | flops 552086016 | bytes 32417872 | solution.py:80
  321.5 7.2 %conditional.2 = ((f32[1,1,2048]{2,1,0:T(1,128)S(1)}, f32[1,1,2048]{2,1,0:T(1,128)S(1)}, f32[1,1,2048,128]{3,2,1,0:T(8,128)S(1)})) conditional(s32[]{:T(128)} %convert_element_type.41, (f32[1,1,2048]{2,1,0:T(1,128)S(1)}, f32[1,1,2048]{2,1,0:T(1,128)S(1)}, f32[1,1,2048,128]{3,2,1,0:T(8,128)S(1)}) %tuple.75, (s32[]{:T(128)}, s32[512]{0:T(512)S(1)}, ...), branch_computations={%region_3.0_spmd, %region_4.6_spmd} | conditional | flops 552086016 | bytes 32417872 | solution.py:80
  328.7 7.2 %conditional.2 = ((f32[1,1,2048]{2,1,0:T(1,128)S(1)}, f32[1,1,2048]{2,1,0:T(1,128)S(1)}, f32[1,1,2048,128]{3,2,1,0:T(8,128)S(1)})) conditional(s32[]{:T(128)} %convert_element_type.41, (f32[1,1,2048]{2,1,0:T(1,128)S(1)}, f32[1,1,2048]{2,1,0:T(1,128)S(1)}, f32[1,1,2048,128]{3,2,1,0:T(8,128)S(1)}) %tuple.75, (s32[]{:T(128)}, s32[512]{0:T(512)S(1)}, ...), branch_computations={%region_3.0_spmd, %region_4.6_spmd} | conditional | flops 552086016 | bytes 32417872 | solution.py:80
  336.0 7.2 %conditional.2 = ((f32[1,1,2048]{2,1,0:T(1,128)S(1)}, f32[1,1,2048]{2,1,0:T(1,128)S(1)}, f32[1,1,2048,128]{3,2,1,0:T(8,128)S(1)})) conditional(s32[]{:T(128)} %convert_element_type.41, (f32[1,1,2048]{2,1,0:T(1,128)S(1)}, f32[1,1,2048]{2,1,0:T(1,128)S(1)}, f32[1,1,2048,128]{3,2,1,0:T(8,128)S(1)}) %tuple.75, (s32[]{:T(128)}, s32[512]{0:T(512)S(1)}, ...), branch_computations={%region_3.0_spmd, %region_4.6_spmd} | conditional | flops 552086016 | bytes 32417872 | solution.py:80
  343.2 7.2 %conditional.2 = ((f32[1,1,2048]{2,1,0:T(1,128)S(1)}, f32[1,1,2048]{2,1,0:T(1,128)S(1)}, f32[1,1,2048,128]{3,2,1,0:T(8,128)S(1)})) conditional(s32[]{:T(128)} %convert_element_type.41, (f32[1,1,2048]{2,1,0:T(1,128)S(1)}, f32[1,1,2048]{2,1,0:T(1,128)S(1)}, f32[1,1,2048,128]{3,2,1,0:T(8,128)S(1)}) %tuple.75, (s32[]{:T(128)}, s32[512]{0:T(512)S(1)}, ...), branch_computations={%region_3.0_spmd, %region_4.6_spmd} | conditional | flops 552086016 | bytes 32417872 | solution.py:80
  350.4 7.2 %conditional.2 = ((f32[1,1,2048]{2,1,0:T(1,128)S(1)}, f32[1,1,2048]{2,1,0:T(1,128)S(1)}, f32[1,1,2048,128]{3,2,1,0:T(8,128)S(1)})) conditional(s32[]{:T(128)} %convert_element_type.41, (f32[1,1,2048]{2,1,0:T(1,128)S(1)}, f32[1,1,2048]{2,1,0:T(1,128)S(1)}, f32[1,1,2048,128]{3,2,1,0:T(8,128)S(1)}) %tuple.75, (s32[]{:T(128)}, s32[512]{0:T(512)S(1)}, ...), branch_computations={%region_3.0_spmd, %region_4.6_spmd} | conditional | flops 552086016 | bytes 32417872 | solution.py:80
  357.7 7.2 %conditional.2 = ((f32[1,1,2048]{2,1,0:T(1,128)S(1)}, f32[1,1,2048]{2,1,0:T(1,128)S(1)}, f32[1,1,2048,128]{3,2,1,0:T(8,128)S(1)})) conditional(s32[]{:T(128)} %convert_element_type.41, (f32[1,1,2048]{2,1,0:T(1,128)S(1)}, f32[1,1,2048]{2,1,0:T(1,128)S(1)}, f32[1,1,2048,128]{3,2,1,0:T(8,128)S(1)}) %tuple.75, (s32[]{:T(128)}, s32[512]{0:T(512)S(1)}, ...), branch_computations={%region_3.0_spmd, %region_4.6_spmd} | conditional | flops 552086016 | bytes 32417872 | solution.py:80
  364.9 7.2 %conditional.2 = ((f32[1,1,2048]{2,1,0:T(1,128)S(1)}, f32[1,1,2048]{2,1,0:T(1,128)S(1)}, f32[1,1,2048,128]{3,2,1,0:T(8,128)S(1)})) conditional(s32[]{:T(128)} %convert_element_type.41, (f32[1,1,2048]{2,1,0:T(1,128)S(1)}, f32[1,1,2048]{2,1,0:T(1,128)S(1)}, f32[1,1,2048,128]{3,2,1,0:T(8,128)S(1)}) %tuple.75, (s32[]{:T(128)}, s32[512]{0:T(512)S(1)}, ...), branch_computations={%region_3.0_spmd, %region_4.6_spmd} | conditional | flops 552086016 | bytes 32417872 | solution.py:80
  372.2 7.2 %conditional.2 = ((f32[1,1,2048]{2,1,0:T(1,128)S(1)}, f32[1,1,2048]{2,1,0:T(1,128)S(1)}, f32[1,1,2048,128]{3,2,1,0:T(8,128)S(1)})) conditional(s32[]{:T(128)} %convert_element_type.41, (f32[1,1,2048]{2,1,0:T(1,128)S(1)}, f32[1,1,2048]{2,1,0:T(1,128)S(1)}, f32[1,1,2048,128]{3,2,1,0:T(8,128)S(1)}) %tuple.75, (s32[]{:T(128)}, s32[512]{0:T(512)S(1)}, ...), branch_computations={%region_3.0_spmd, %region_4.6_spmd} | conditional | flops 552086016 | bytes 32417872 | solution.py:80
  379.4 7.2 %conditional.2 = ((f32[1,1,2048]{2,1,0:T(1,128)S(1)}, f32[1,1,2048]{2,1,0:T(1,128)S(1)}, f32[1,1,2048,128]{3,2,1,0:T(8,128)S(1)})) conditional(s32[]{:T(128)} %convert_element_type.41, (f32[1,1,2048]{2,1,0:T(1,128)S(1)}, f32[1,1,2048]{2,1,0:T(1,128)S(1)}, f32[1,1,2048,128]{3,2,1,0:T(8,128)S(1)}) %tuple.75, (s32[]{:T(128)}, s32[512]{0:T(512)S(1)}, ...), branch_computations={%region_3.0_spmd, %region_4.6_spmd} | conditional | flops 552086016 | bytes 32417872 | solution.py:80
  386.7 7.2 %conditional.2 = ((f32[1,1,2048]{2,1,0:T(1,128)S(1)}, f32[1,1,2048]{2,1,0:T(1,128)S(1)}, f32[1,1,2048,128]{3,2,1,0:T(8,128)S(1)})) conditional(s32[]{:T(128)} %convert_element_type.41, (f32[1,1,2048]{2,1,0:T(1,128)S(1)}, f32[1,1,2048]{2,1,0:T(1,128)S(1)}, f32[1,1,2048,128]{3,2,1,0:T(8,128)S(1)}) %tuple.75, (s32[]{:T(128)}, s32[512]{0:T(512)S(1)}, ...), branch_computations={%region_3.0_spmd, %region_4.6_spmd} | conditional | flops 552086016 | bytes 32417872 | solution.py:80
  393.9 7.2 %conditional.2 = ((f32[1,1,2048]{2,1,0:T(1,128)S(1)}, f32[1,1,2048]{2,1,0:T(1,128)S(1)}, f32[1,1,2048,128]{3,2,1,0:T(8,128)S(1)})) conditional(s32[]{:T(128)} %convert_element_type.41, (f32[1,1,2048]{2,1,0:T(1,128)S(1)}, f32[1,1,2048]{2,1,0:T(1,128)S(1)}, f32[1,1,2048,128]{3,2,1,0:T(8,128)S(1)}) %tuple.75, (s32[]{:T(128)}, s32[512]{0:T(512)S(1)}, ...), branch_computations={%region_3.0_spmd, %region_4.6_spmd} | conditional | flops 552086016 | bytes 32417872 | solution.py:80
  401.2 7.2 %conditional.2 = ((f32[1,1,2048]{2,1,0:T(1,128)S(1)}, f32[1,1,2048]{2,1,0:T(1,128)S(1)}, f32[1,1,2048,128]{3,2,1,0:T(8,128)S(1)})) conditional(s32[]{:T(128)} %convert_element_type.41, (f32[1,1,2048]{2,1,0:T(1,128)S(1)}, f32[1,1,2048]{2,1,0:T(1,128)S(1)}, f32[1,1,2048,128]{3,2,1,0:T(8,128)S(1)}) %tuple.75, (s32[]{:T(128)}, s32[512]{0:T(512)S(1)}, ...), branch_computations={%region_3.0_spmd, %region_4.6_spmd} | conditional | flops 552086016 | bytes 32417872 | solution.py:80
  408.4 7.2 %conditional.2 = ((f32[1,1,2048]{2,1,0:T(1,128)S(1)}, f32[1,1,2048]{2,1,0:T(1,128)S(1)}, f32[1,1,2048,128]{3,2,1,0:T(8,128)S(1)})) conditional(s32[]{:T(128)} %convert_element_type.41, (f32[1,1,2048]{2,1,0:T(1,128)S(1)}, f32[1,1,2048]{2,1,0:T(1,128)S(1)}, f32[1,1,2048,128]{3,2,1,0:T(8,128)S(1)}) %tuple.75, (s32[]{:T(128)}, s32[512]{0:T(512)S(1)}, ...), branch_computations={%region_3.0_spmd, %region_4.6_spmd} | conditional | flops 552086016 | bytes 32417872 | solution.py:80
  415.7 7.2 %conditional.2 = ((f32[1,1,2048]{2,1,0:T(1,128)S(1)}, f32[1,1,2048]{2,1,0:T(1,128)S(1)}, f32[1,1,2048,128]{3,2,1,0:T(8,128)S(1)})) conditional(s32[]{:T(128)} %convert_element_type.41, (f32[1,1,2048]{2,1,0:T(1,128)S(1)}, f32[1,1,2048]{2,1,0:T(1,128)S(1)}, f32[1,1,2048,128]{3,2,1,0:T(8,128)S(1)}) %tuple.75, (s32[]{:T(128)}, s32[512]{0:T(512)S(1)}, ...), branch_computations={%region_3.0_spmd, %region_4.6_spmd} | conditional | flops 552086016 | bytes 32417872 | solution.py:80
  422.9 7.2 %conditional.2 = ((f32[1,1,2048]{2,1,0:T(1,128)S(1)}, f32[1,1,2048]{2,1,0:T(1,128)S(1)}, f32[1,1,2048,128]{3,2,1,0:T(8,128)S(1)})) conditional(s32[]{:T(128)} %convert_element_type.41, (f32[1,1,2048]{2,1,0:T(1,128)S(1)}, f32[1,1,2048]{2,1,0:T(1,128)S(1)}, f32[1,1,2048,128]{3,2,1,0:T(8,128)S(1)}) %tuple.75, (s32[]{:T(128)}, s32[512]{0:T(512)S(1)}, ...), branch_computations={%region_3.0_spmd, %region_4.6_spmd} | conditional | flops 552086016 | bytes 32417872 | solution.py:80
  430.2 7.2 %conditional.2 = ((f32[1,1,2048]{2,1,0:T(1,128)S(1)}, f32[1,1,2048]{2,1,0:T(1,128)S(1)}, f32[1,1,2048,128]{3,2,1,0:T(8,128)S(1)})) conditional(s32[]{:T(128)} %convert_element_type.41, (f32[1,1,2048]{2,1,0:T(1,128)S(1)}, f32[1,1,2048]{2,1,0:T(1,128)S(1)}, f32[1,1,2048,128]{3,2,1,0:T(8,128)S(1)}) %tuple.75, (s32[]{:T(128)}, s32[512]{0:T(512)S(1)}, ...), branch_computations={%region_3.0_spmd, %region_4.6_spmd} | conditional | flops 552086016 | bytes 32417872 | solution.py:80
  437.4 7.2 %conditional.2 = ((f32[1,1,2048]{2,1,0:T(1,128)S(1)}, f32[1,1,2048]{2,1,0:T(1,128)S(1)}, f32[1,1,2048,128]{3,2,1,0:T(8,128)S(1)})) conditional(s32[]{:T(128)} %convert_element_type.41, (f32[1,1,2048]{2,1,0:T(1,128)S(1)}, f32[1,1,2048]{2,1,0:T(1,128)S(1)}, f32[1,1,2048,128]{3,2,1,0:T(8,128)S(1)}) %tuple.75, (s32[]{:T(128)}, s32[512]{0:T(512)S(1)}, ...), branch_computations={%region_3.0_spmd, %region_4.6_spmd} | conditional | flops 552086016 | bytes 32417872 | solution.py:80
  444.7 7.2 %conditional.2 = ((f32[1,1,2048]{2,1,0:T(1,128)S(1)}, f32[1,1,2048]{2,1,0:T(1,128)S(1)}, f32[1,1,2048,128]{3,2,1,0:T(8,128)S(1)})) conditional(s32[]{:T(128)} %convert_element_type.41, (f32[1,1,2048]{2,1,0:T(1,128)S(1)}, f32[1,1,2048]{2,1,0:T(1,128)S(1)}, f32[1,1,2048,128]{3,2,1,0:T(8,128)S(1)}) %tuple.75, (s32[]{:T(128)}, s32[512]{0:T(512)S(1)}, ...), branch_computations={%region_3.0_spmd, %region_4.6_spmd} | conditional | flops 552086016 | bytes 32417872 | solution.py:80
  451.9 7.2 %conditional.2 = ((f32[1,1,2048]{2,1,0:T(1,128)S(1)}, f32[1,1,2048]{2,1,0:T(1,128)S(1)}, f32[1,1,2048,128]{3,2,1,0:T(8,128)S(1)})) conditional(s32[]{:T(128)} %convert_element_type.41, (f32[1,1,2048]{2,1,0:T(1,128)S(1)}, f32[1,1,2048]{2,1,0:T(1,128)S(1)}, f32[1,1,2048,128]{3,2,1,0:T(8,128)S(1)}) %tuple.75, (s32[]{:T(128)}, s32[512]{0:T(512)S(1)}, ...), branch_computations={%region_3.0_spmd, %region_4.6_spmd} | conditional | flops 552086016 | bytes 32417872 | solution.py:80
  460.2 7.6 %all-to-all-start.1 = ((bf16[32,64,128]{2,1,0:T(8,128)(2,1)}), bf16[32,64,128]{2,1,0:T(8,128)(2,1)S(1)}, u32[]{:S(2)}, u32[]{:S(2)}) async-start(bf16[32,64,128]{2,1,0:T(8,128)(2,1)} %bitcast.18), calls=%async_computation.1 | async-start | bytes 1048576 | tf_op jit(solution)/shard_map/all_to_all | solution.py:90
  468.7 10.7 %all-to-all-done.1 = bf16[32,64,128]{2,1,0:T(8,128)(2,1)S(1)} async-done(((bf16[32,64,128]{2,1,0:T(8,128)(2,1)}), bf16[32,64,128]{2,1,0:T(8,128)(2,1)S(1)}, u32[]{:S(2)}, u32[]{:S(2)}) %all-to-all-start.1) | async-done | bytes 524320 | tf_op jit(solution)/shard_map/all_to_all | solution.py:90
  (331 shorter events, 222.2 us)
Async XLA Ops:
  7.2 219.9 %all-gather.2.cloned.1.call-start = ((), (), s32[]{:S(2)}) async-start(), calls=%async_computation.2 | async-start | bytes 9437184 | tf_op jit(solution)/shard_map/all_gather | solution.py:70
  227.2 240.7 %copy-start = (bf16[64,4096]{1,0:T(8,128)(2,1)S(1)}, bf16[64,4096]{1,0:T(8,128)(2,1)}, u32[]{:S(2)}) copy-start(bf16[64,4096]{1,0:T(8,128)(2,1)} %param.14) | copy-start | bytes 1572868
  460.2 19.2 %all-to-all-start.1 = ((bf16[32,64,128]{2,1,0:T(8,128)(2,1)}), bf16[32,64,128]{2,1,0:T(8,128)(2,1)S(1)}, u32[]{:S(2)}, u32[]{:S(2)}) async-start(bf16[32,64,128]{2,1,0:T(8,128)(2,1)} %bitcast.18), calls=%async_computation.1 | async-start | bytes 1048576 | tf_op jit(solution)/shard_map/all_to_all | solution.py:90
Sparse Core Ops, SparseCore 0:
  137.8 89.2 all-gather.1
where the time goes:
time: 488 us; the launch traced here: 487 us
  local copies, waits for them, and re-layouts  152 us (31%)
  blocking collectives  103 us (21%)
  waiting for transfers between devices  93.9 us (19%)
  matrix products  73.8 us (15%)
  other arithmetic  39.4 us (8%)
  between operations  14.1 us (3%)
  starting transfers between devices  7.61 us (2%)
    slice x32, local copies, waits for them, and re-layouts, step(): v_block = lax.dynamic_slice_in_dim(piece[1], turn * sub_rows, sub_rows, 1)  121 us
    all_gather x1, waiting for transfers between devices, shards(): piece = lax.all_gather(kv_pair, 'blk', axis=2, tiled=True)  83.1 us
    psum x1, blocking collectives, shards(): key_mean = lax.psum(jnp.sum(keys32, axis=0), ('blk', 'uly')) / total_rows  75.8 us
    dot_general x32, matrix products, update(): jnp.einsum('hqk,hkd->hqd', weights.astype(jnp.bfloat16), v_block, preferr...  49.6 us
    reduce_sum x32, other arithmetic, update(): new_sum = run_sum[:, index] * factor + jnp.sum(weights, axis=2)  32.1 us
    all_to_all x1, blocking collectives, shards(): lax.all_to_all(stacked, 'uly', split_axis=2, concat_axis=1, tiled=True)  26.7 us
    dot_general x32, matrix products, update(): jnp.einsum('hqd,hkd->hqk', q_piece, k_block, preferred_element_type=jnp.f...  24.2 us
    unnamed x4, local copies, waits for them, and re-layouts  10.9 us
  transfers between devices with their start and end apart: 2, of which 2 were waited for; matrix products, arithmetic and copies ran while one was open for 1% of the time, Pallas kernels for 0%

commit v1 on v0

v1 whole, which is shorter than its diff:
```python
import functools
import math

import jax
import jax.numpy as jnp
from jax import lax
from jax.experimental import pallas as pl
from jax.experimental.pallas import tpu as pltpu
from jax.sharding import Mesh, PartitionSpec as P

HD = 128
SCALE = 1.0 / math.sqrt(HD)
NZ, NX, NY, NC = 8, 4, 4, 2
T = 64
TOKENS = NZ * NX * NY * NC * T
SRC = NZ * NY
ROWS = SRC * T
TAIL = 16
G = NY * T
LOW, HIGH = 1e-25, 1e25
ALL = ("z", "x", "y", "core")
VMEM = pl.BlockSpec(memory_space=pltpu.VMEM)
ANY = pl.BlockSpec(memory_space=pl.ANY)


def dot_t(a, b):
    return lax.dot_general(a, b, (((1,), (1,)), ((), ())), preferred_element_type=jnp.float32)


def key_mean(sums_ref):
    return jnp.sum(sums_ref[...], axis=0, keepdims=True) / TOKENS


def column(z, x):
    return jnp.where(z % 2 == 0, x, NX - 1 - x)


def thirds(value):
    high = value.astype(jnp.bfloat16).astype(jnp.float32)
    mid = (value - high).astype(jnp.bfloat16).astype(jnp.float32)
    return high, mid, value - high - mid


def tail_rows(value, rows):
    which = lax.broadcasted_iota(jnp.int32, (rows, value.shape[1]), 0)
    high, mid, low = (jnp.broadcast_to(v, which.shape) for v in thirds(value))
    picked = jnp.where(which == 1, mid, jnp.where(which == 2, low, 0.0))
    return jnp.where(which == 0, high, picked).astype(jnp.bfloat16)


def copies(z, srcs, kc, vc, sems):
    out = []
    for s, halves in enumerate(srcs):
        n = NZ // len(halves)
        part = halves[z // n].at[pl.ds(z % n * NY, NY)]
        out.append(pltpu.make_async_copy(part.at[:, 0], kc.at[z, s], sems.at[z]))
        out.append(pltpu.make_async_copy(part.at[:, 1], vc.at[z, s], sems.at[z]))
    return out


def fetch(srcs, kc, vc, sems):
    for z in range(NZ):
        for copy in copies(z, srcs, kc, vc, sems):
            copy.start()


def ready(groups, mean, srcs, kc, vc, sems):
    for z in groups:
        for copy in copies(z, srcs, kc, vc, sems):
            copy.wait()

    @pl.loop(groups[0], groups[-1] + 1)
    def _(z):
        kc[z] = (kc[z].astype(jnp.float32) - mean).astype(jnp.bfloat16)


def attend(q, kc, vc, acc, tot, z, nz, kz, nk, first=0, count=None, mask=None):
    count = kc.shape[1] if count is None else count
    keys = nk * count * G
    at = pl.ds(pl.multiple_of(z * G, G), nz * G)
    ks = (pl.ds(kz, nk), pl.ds(first, count))
    p = jnp.exp(dot_t(q[at], kc[ks].reshape(keys, HD)) * SCALE)
    if mask is not None:
        p = jnp.where(mask, p, 0.0)
    part = p[:, :HD]
    for i in range(1, keys // HD):
        part = part + p[:, i * HD : (i + 1) * HD]
    tot[at] += part
    acc[at] += jnp.dot(
        p.astype(jnp.bfloat16), vc[ks].reshape(keys, HD), preferred_element_type=jnp.float32
    )


def work(mean, srcs, others, sems, q, kc, vc, acc, tot, mask=None):
    ns = len(srcs)
    refs = (q, kc, vc, acc, tot)
    ready(range(NZ // 2), mean, srcs, kc, vc, sems)
    nk = 8 // ns

    @pl.loop(0, 2 * (4 // nk))
    def _(i):
        attend(*refs, 4 + i % 2 * 2, 2, i // 2 * nk, nk)

    ready(range(NZ // 2, NZ), mean, srcs, kc, vc, sems)

    @pl.loop(0, 2)
    def _(i):
        attend(*refs, i * 4 + 2, 2, i * 4, 2)

    @pl.loop(0, 2)
    def _(i):
        for j in range(2):
            z = 4 * i + 2 * j
            attend(*refs, z + 1, 1, z, 1)

    if mask is not None:

        @pl.loop(0, 2)
        def _(i):
            for j in range(4):
                z = 4 * i + j
                attend(*refs, z, 1, z, 1, 0, 2, mask)

    z, x = lax.axis_index("z"), lax.axis_index("x")
    for first, shift in others:
        later = column(z, (x + shift) % NX) > column(z, x)
        odd = later.astype(jnp.int32)

        @pl.loop(0, 1)
        def _(i):
            for j in range(4):
                at = 4 * i + 2 * j + odd
                attend(*refs, at, 1, at, 1, first, 2)


def first_kernel(sums, q, o0, o1, l0, l1, acc, tot, kc, vc, sems):
    core = lax.axis_index("core")
    srcs = ([o0], [o1], [l0], [l1])
    fetch(srcs, kc, vc, sems)
    acc[...] = jnp.zeros_like(acc)
    tot[...] = jnp.zeros_like(tot)
    shape = (G, 2 * G)
    col = lax.broadcasted_iota(jnp.int32, shape, 1)
    kpos = (col % G) // T * (NC * T) + (core + col // G) % NC * T + col % T
    row = lax.broadcasted_iota(jnp.int32, shape, 0)
    qpos = row // T * (NC * T) + core * T + row % T
    work(key_mean(sums), srcs, [(2, NX - 1)], sems, q, kc, vc, acc, tot, kpos <= qpos)


def second_kernel(sums, q, r0, r1, acc_in, tot_in, acc, tot, kc, vc, sems, acc0, tot0, sem):
    srcs = ([r0], [r1])
    fetch(srcs, kc, vc, sems)
    state = state_in(acc_in, tot_in, acc0, tot0, sem)
    acc[...] = jnp.zeros_like(acc)
    tot[...] = jnp.zeros_like(tot)
    work(key_mean(sums), srcs, [(0, 1)], sems, q, kc, vc, acc, tot)
    for copy in state:
        copy.wait()
    acc[...] += acc0[...]
    tot[...] += tot0[...]


def state_in(acc_in, tot_in, acc0, tot0, sem):
    pair = [
        pltpu.make_async_copy(acc_in, acc0, sem.at[0]),
        pltpu.make_async_copy(tot_in, tot0, sem.at[1]),
    ]
    for copy in pair:
        copy.start()
    return pair


def robust(sums, q, srcs, out, acc, run_max, run_sum, stage):
    dz, x, core = lax.axis_index("z"), lax.axis_index("x"), lax.axis_index("core")
    mean = key_mean(sums)
    acc[...] = jnp.zeros_like(acc)
    run_sum[...] = jnp.zeros_like(run_sum)
    run_max[...] = jnp.full_like(run_max, -1e30)
    for s, halves in enumerate(srcs):
        kx = column(dz, (x + (0, NX - 1, 1, 2)[s // 2]) % NX)
        kcore = (core + s % 2) % NC
        n = SRC // len(halves)
        for h, src in enumerate(halves):
            pltpu.sync_copy(src, stage.at[pl.ds(h * n, n)])

        def block(i, carry):
            z, kz = i // NZ, i % NZ

            @pl.when(kz <= z)
            def _():
                at = pl.ds(pl.multiple_of(z * G, G), G)
                part = stage[pl.ds(kz * NY, NY)]
                k = (part[:, 0].reshape(G, HD).astype(jnp.float32) - mean).astype(jnp.bfloat16)
                scores = dot_t(q[at], k) * SCALE
                row = lax.broadcasted_iota(jnp.int32, (G, G), 0)
                col = lax.broadcasted_iota(jnp.int32, (G, G), 1)
                qpos = ((z * NX + column(z, column(dz, x))) * NY + row // T) * NC * T + core * T + row % T
                kpos = ((kz * NX + column(kz, kx)) * NY + col // T) * NC * T + kcore * T + col % T
                mask = kpos <= qpos
                old = run_max[at]
                new = jnp.maximum(
                    old, jnp.max(jnp.where(mask, scores, -1e30), axis=1, keepdims=True)
                )
                w = jnp.where(mask, jnp.exp(scores - new[:, :1]), 0.0)
                factor = jnp.exp(old - new)
                run_sum[at] = run_sum[at] * factor + jnp.sum(w, axis=1, keepdims=True)
                acc[at] = acc[at] * factor + jnp.dot(
                    w.astype(jnp.bfloat16),
                    part[:, 1].reshape(G, HD),
                    preferred_element_type=jnp.float32,
                )
                run_max[at] = new

            return carry

        lax.fori_loop(0, NZ * NZ, block, 0)
    out[:, :T] = (acc[...] / run_sum[...]).astype(jnp.bfloat16).reshape(SRC, T, HD)


def far_kernel(
    sums, q, a0, b0, a1, b1, acc_in, tot_in, o0, o1, l0, l1, r0, r1,
    out, acc, tot, kc, vc, sems, acc0, tot0, sem, stage,
):
    far = ([a0, b0], [a1, b1])
    fetch(far, kc, vc, sems)
    state = state_in(acc_in, tot_in, acc0, tot0, sem)
    acc[...] = jnp.zeros_like(acc)
    tot[...] = jnp.zeros_like(tot)
    work(key_mean(sums), far, [(0, 2)], sems, q, kc, vc, acc, tot)
    for copy in state:
        copy.wait()
    acc[...] += acc0[...]
    tot[...] += tot0[...]
    total = jnp.sum(tot[...], axis=1, keepdims=True)
    out[:, :T] = (acc[...] / total).astype(jnp.bfloat16).reshape(SRC, T, HD)
    tail = tail_rows(key_mean(sums), TAIL)
    out[:, T:] = jnp.broadcast_to(tail[None], (SRC, TAIL, HD))
    fine = jnp.where((total > LOW) & (total < HIGH), 0.0, 1.0)

    @pl.when(jnp.max(fine) > 0.0)
    def _():
        robust(sums, q, ([o0], [o1], [l0], [l1], [r0], [r1], *far), out, acc, acc0, tot, stage)


STATE = jax.ShapeDtypeStruct((ROWS, HD), jnp.float32)


def call(kernel, name, ins, outs, scratch, units):
    return functools.partial(
        pl.pallas_call(
            kernel,
            name=name,
            in_specs=ins,
            out_specs=[VMEM] * len(outs),
            out_shape=outs,
            scratch_shapes=scratch,
            compiler_params=pltpu.CompilerParams(vmem_limit_bytes=48 << 20),
            cost_estimate=pl.CostEstimate(
                flops=units * 32 * G * 2 * G * HD, bytes_accessed=4 << 20, transcendentals=0
            ),
        )
    )


def shards(queries, keys, values):
    def by_head(a):
        return a.reshape(T, SRC, HD).transpose(1, 0, 2)

    groups = [
        [
            ((z * NX + (x if z % 2 == 0 else NX - 1 - x)) * NY + y) * NC + core
            for z in range(NZ)
            for y in range(NY)
        ]
        for x in range(NX)
        for core in range(NC)
    ]

    def exchange(a):
        return lax.all_to_all(a, ALL, 0, 0, axis_index_groups=groups, tiled=True)

    kv = jnp.stack([by_head(keys), by_head(values)], axis=1)
    with jax.named_scope("kv_to_heads"):
        own = exchange(kv)
    queries, _ = lax.optimization_barrier((by_head(queries), own))
    with jax.named_scope("q_to_heads"):
        q = exchange(queries).reshape(ROWS, HD)
    right = [(i, (i + 1) % NX) for i in range(NX)]
    left = [(i, (i - 1) % NX) for i in range(NX)]
    across = [(i, (i + 2) % NX) for i in range(NX)]
    swap = [(0, 1), (1, 0)]
    half = SRC // 2
    with jax.named_scope("key_sums"):
        sums = jnp.sum(own[:, 0].astype(jnp.float32), axis=(0, 1))[None]
        sums = sums + lax.ppermute(sums, "core", swap)
        sums = jnp.concatenate([sums] + [lax.ppermute(sums, "x", p) for p in (right, left, across)])
    with jax.named_scope("ring"):
        l0 = lax.ppermute(own, "x", right)
        r0 = lax.ppermute(own, "x", left)
        o1 = lax.ppermute(own, "core", swap)
        l0, r0, q, sums = lax.optimization_barrier((l0, r0, q, sums))
        l1 = lax.ppermute(l0, "core", swap)
        r1 = lax.ppermute(r0, "core", swap)
        a0 = lax.ppermute(l0[:half], "x", right)
        b0 = lax.ppermute(r0[half:], "x", left)

    def bufs(ns):
        return [pltpu.VMEM((NZ, ns, NY, T, HD), jnp.bfloat16)] * 2 + [
            pltpu.SemaphoreType.DMA((NZ,))
        ]

    state = [pltpu.VMEM((ROWS, HD), jnp.float32)] * 2
    first = [VMEM] * 2 + [ANY] * 4
    acc, tot = call(first_kernel, "first", first, [STATE] * 2, bufs(4), 76)(sums, q, own, o1, l0, l1)
    a0, b0, acc, tot = lax.optimization_barrier((a0, b0, acc, tot))
    with jax.named_scope("ring"):
        a1 = lax.ppermute(a0, "core", swap)
        b1 = lax.ppermute(b0, "core", swap)
    acc, tot = call(
        second_kernel,
        "second",
        first,
        [STATE] * 2,
        bufs(2) + state + [pltpu.SemaphoreType.DMA((2,))],
        32,
    )(sums, q, r0, r1, acc, tot)
    (out,) = call(
        far_kernel,
        "far",
        [VMEM] * 2 + [ANY] * 12,
        [jax.ShapeDtypeStruct((SRC, T + TAIL, HD), jnp.bfloat16)],
        state
        + bufs(2)
        + state
        + [pltpu.SemaphoreType.DMA((2,)), pltpu.VMEM((SRC, 2, T, HD), jnp.bfloat16)],
        32,
    )(sums, q, a0, b0, a1, b1, acc, tot, own, o1, l0, l1, r0, r1)
    with jax.named_scope("home"):
        home = exchange(out)
    attended = home[:, :T].transpose(1, 0, 2).reshape(T, SRC * HD)
    parts = home[:, T : T + 3].astype(jnp.float32)
    mean = (parts[:, 0] + parts[:, 1] + parts[:, 2]).reshape(SRC * HD)
    key_cache = (keys.astype(jnp.float32) - mean).astype(jnp.bfloat16)
    return attended, key_cache


def solution(mesh):
    split = Mesh(mesh.devices.reshape(NZ, NX, NY, NC), ALL)
    spec = P(ALL, None)
    return jax.shard_map(
        shards, mesh=split, in_specs=(spec,) * 3, out_specs=(spec,) * 2, check_vma=False
    )
```

time: 488 us -> 308 us (0.63)
  the two profiles are of different devices: /device:TPU:225 before, /device:TPU:1 now
where the time goes in v1:
time: 308 us
  Pallas kernels  200 us (65%)
  blocking collectives  63.8 us (21%)
  starting transfers between devices  22.9 us (7%)
  waiting for transfers between devices  11.4 us (4%)
  local copies, waits for them, and re-layouts  7.2 us (2%)
    pallas_call x1, Pallas kernels, shards(): call(far_kernel, 'far', [VMEM] * 2 + [ANY] * 12, [jax.ShapeDtypeStruct((S...  177 us
    all_to_all x2, blocking collectives, exchange(): return lax.all_to_all(a, ALL, 0, 0, axis_index_groups=groups, tiled=True)  63.8 us
    pallas_call x1, Pallas kernels, shards(): call(first_kernel, 'first', first, [STATE] * 2, bufs(4), 76)  15.2 us
    ppermute x3, waiting for transfers between devices, shards(): lax.ppermute(sums, 'x', p)  10.6 us
    pallas_call x1, Pallas kernels, shards(): call(second_kernel, 'second', first, [STATE] * 2, bufs(2) + state + [pltp...  7.97 us
    all_to_all x1, starting transfers between devices, exchange(): return lax.all_to_all(a, ALL, 0, 0, axis_index_groups=groups, tiled=True)  7.44 us
  transfers between devices with their start and end apart: 14, of which 4 were waited for; matrix products, arithmetic and copies ran while one was open for 1% of the time, Pallas kernels for 8%

profile of v1, /device:TPU:1, one launch (start us, length us, event | category | flops | bytes accessed | tf_op | source)
XLA Modules:
  0.0 307.7 jit_solution(13734730154630966225)
XLA Ops:
  0.6 0.0 copy-start
  0.6 1.0 copy-done
  1.7 1.3 bitcast_bitcast_fusion.1
  3.0 0.1 pad_maximum_fusion
  3.1 0.0 copy-start.6
  3.1 41.2 %all_to_all.15.o0 = bf16[32,2,64,128]{3,2,1,0:T(8,128)(2,1)S(1)} all-to-all(bf16[32,2,64,128]{3,2,1,0:T(8,128)(2,1)S(1)} %pad_maximum_fusion), channel_id=1, replica_groups={{0,2,4,6,56,58,60,62,64,66,68,70,120,122,124,126,128,130,132,134,184,18..., dimensions={0} | all-to-all | bytes 2097152 | tf_op jit(solution)/shard_map/kv_to_heads/all_to_all | solution.py:280
  44.4 0.0 collective-permute-start.1
  44.4 1.5 collective-permute-start
  45.8 0.0 copy-done.6
  45.8 0.9 bitcast_bitcast_fusion
  46.8 7.4 %all-to-all-start.1 = ((bf16[32,64,128]{2,1,0:T(8,128)(2,1)}), bf16[32,64,128]{2,1,0:T(8,128)(2,1)S(1)}, u32[]{:S(2)}, u32[]{:S(2)}) async-start(bf16[32,64,128]{2,1,0:T(8,128)(2,1)} %bitcast_bitcast_fusion), calls=%async_computation.1 | async-start | bytes 1048576 | tf_op jit(solution)/shard_map/q_to_heads/all_to_all | solution.py:280
  54.2 0.3 convert_reduce_fusion
  54.5 2.7 collective-permute-start.2
  57.2 0.8 collective-permute-done.2
  58.0 0.0 collective-permute-start.5
  58.0 1.5 collective-permute-start.4
  59.5 0.6 collective-permute-start.3
  60.1 6.5 %collective-permute-done.5 = f32[1,128]{1,0:T(1,128)S(1)} collective-permute-done((f32[1,128]{1,0:T(1,128)S(1)}, f32[1,128]{1,0:T(1,128)S(1)}, u32[]{:S(2)}, u32[]{:S(2)}) %collective-permute-start.5) | collective-permute-done | bytes 544 | tf_op jit(solution)/shard_map/key_sums/ppermute | solution.py:296
  66.6 2.8 collective-permute-start.8
  69.4 0.6 collective-permute-done.4
  70.0 3.5 %collective-permute-done.3 = f32[1,128]{1,0:T(1,128)S(1)} collective-permute-done((f32[1,128]{1,0:T(1,128)S(1)}, f32[1,128]{1,0:T(1,128)S(1)}, u32[]{:S(2)}, u32[]{:S(2)}) %collective-permute-start.3) | collective-permute-done | bytes 544 | tf_op jit(solution)/shard_map/key_sums/ppermute | solution.py:296
  73.5 0.0 all-to-all-done.1
  73.5 0.0 collective-permute-done.1.r0
  73.5 0.0 copy-start.2
  73.5 0.0 collective-permute-done.l0
  73.5 3.5 %collective-permute-start.9 = (bf16[32,2,64,128]{3,2,1,0:T(8,128)(2,1)}, bf16[32,2,64,128]{3,2,1,0:T(8,128)(2,1)S(1)}, u32[]{:S(2)}, u32[]{:S(2)}) collective-permute-start(bf16[32,2,64,128]{3,2,1,0:T(8,128)(2,1)} %collective-permute-done.l0), channel_id=1, source_target_pairs={{0,1},{1,0},{2,3},{3,2},{4,5},{5,4},{6,7},{7,6},{8,9},{9,8},{10,11... | collective-permute-start | bytes 3145736 | tf_op jit(solution)/shard_map/ring/ppermute | solution.py:302
  77.0 1.1 slice.25
  78.2 0.4 collective-permute-start.12
  78.5 0.0 collective-permute-start.7
  78.5 1.5 collective-permute-start.6
  80.0 0.0 collective-permute-done.8.o1
  80.0 0.0 collective-permute-done.9.l1
  80.0 1.0 copy-done.7
  81.0 15.2 %first.1 = (f32[2048,128]{1,0:T(8,128)S(1)}, f32[2048,128]{1,0:T(8,128)S(1)}) custom-call(f32[4,128]{1,0:T(4,128)S(1)} %pad_maximum_fusion.1.sums, bf16[2048,128]{1,0:T(8,128)(2,1)S(1)} %bitcast.35, bf16[32,2,64,128]{3,2,1,0:T(8,128)(2,1)S(1)} %all_to_all.15.o0, bf16[32,2,64,128]{3,2,1,0:T(8,128)(2,1)} %collective-permute-done.8.o1, ...), custom_call_target="tpu_custom_call" | custom-call | flops 40802189312 | bytes 4194304 | tf_op jit(solution)/shard_map/first/pallas_call | solution.py:314
  96.2 1.0 copy-done.4
  97.1 0.0 collective-permute-done.7.b0
  97.1 0.0 collective-permute-done.6.a0
  97.1 0.8 collective-permute-start.10
  97.9 0.3 collective-permute-start.11
  98.2 0.0 collective-permute-done.12.r1
  98.3 8.0 %second.1 = (f32[2048,128]{1,0:T(8,128)S(1)}, f32[2048,128]{1,0:T(8,128)S(1)}) custom-call(f32[4,128]{1,0:T(4,128)S(1)} %pad_maximum_fusion.1.sums, bf16[2048,128]{1,0:T(8,128)(2,1)S(1)} %bitcast.36, bf16[32,2,64,128]{3,2,1,0:T(8,128)(2,1)S(1)} %collective-permute-done.1.r0, bf16[32,2,64,128]{3,2,1,0:T(8,128)(2,1)S(1)} %collective-permute-done.12.r1, ...), custom_call_target="tpu_custom_call" | custom-call | flops 17179869184 | bytes 4194304 | tf_op jit(solution)/shard_map/second/pallas_call | solution.py:319
  106.2 0.0 collective-permute-done.10.a1
  106.2 0.0 collective-permute-done.11.b1
  106.3 177.1 %far.1 = bf16[32,80,128]{2,1,0:T(8,128)(2,1)S(1)} custom-call(f32[4,128]{1,0:T(4,128)S(1)} %pad_maximum_fusion.1.sums, bf16[2048,128]{1,0:T(8,128)(2,1)S(1)} %bitcast.37, bf16[16,2,64,128]{3,2,1,0:T(8,128)(2,1)S(1)} %collective-permute-done.6.a0, bf16[16,2,64,128]{3,2,1,0:T(8,128)(2,1)S(1)} %collective-permute-done.7.b0, ...), custom_call_target="tpu_custom_call" | custom-call | flops 17179869184 | bytes 4194304 | tf_op jit(solution)/shard_map/far/pallas_call | solution.py:327
  283.4 0.0 copy-start.5
  283.4 22.5 %all_to_all.16 = bf16[32,80,128]{2,1,0:T(8,128)(2,1)S(1)} all-to-all(bf16[32,80,128]{2,1,0:T(8,128)(2,1)S(1)} %far.1), channel_id=1, replica_groups={{0,2,4,6,56,58,60,62,64,66,68,70,120,122,124,126,128,130,132,134,184,18..., dimensions={0} | all-to-all | bytes 1310720 | tf_op jit(solution)/shard_map/home/all_to_all | solution.py:280
  306.0 0.9 subtract_convert_fusion
  306.9 0.8 copy_bitcast_fusion
  (13 shorter events, 0.1 us)
Async XLA Ops:
  0.6 1.0 copy-start
  3.1 42.7 %copy-start.6 = (bf16[64,4096]{1,0:T(8,128)(2,1)S(1)}, bf16[64,4096]{1,0:T(8,128)(2,1)}, u32[]{:S(2)}) copy-start(bf16[64,4096]{1,0:T(8,128)(2,1)} %param.3) | copy-start | bytes 1572868
  44.4 35.6 %copy-start.1 = (bf16[32,2,64,128]{3,2,1,0:T(8,128)(2,1)}, bf16[32,2,64,128]{3,2,1,0:T(8,128)(2,1)S(1)}, u32[]{:S(2)}) copy-start(bf16[32,2,64,128]{3,2,1,0:T(8,128)(2,1)S(1)} %all_to_all.15.o0) | copy-start | bytes 3145732
  44.4 29.1 %collective-permute-start.1 = (bf16[32,2,64,128]{3,2,1,0:T(8,128)(2,1)S(1)}, bf16[32,2,64,128]{3,2,1,0:T(8,128)(2,1)S(1)}, u32[]{:S(2)}, u32[]{:S(2)}) collective-permute-start(bf16[32,2,64,128]{3,2,1,0:T(8,128)(2,1)S(1)} %all_to_all.15.o0), channel_id=1, source_target_pairs={{0,24},{8,0},{16,8},{24,16},{1,25},{9,1},{17,9},{25,17},{2,26},{10... | collective-permute-start | bytes 3145736 | tf_op jit(solution)/shard_map/ring/ppermute | solution.py:299
  44.4 29.2 %collective-permute-start = (bf16[32,2,64,128]{3,2,1,0:T(8,128)(2,1)S(1)}, bf16[32,2,64,128]{3,2,1,0:T(8,128)(2,1)}, u32[]{:S(2)}, u32[]{:S(2)}) collective-permute-start(bf16[32,2,64,128]{3,2,1,0:T(8,128)(2,1)S(1)} %all_to_all.15.o0), channel_id=1, source_target_pairs={{0,8},{8,16},{16,24},{24,0},{1,9},{9,17},{17,25},{25,1},{2,10},{10... | collective-permute-start | bytes 3145736 | tf_op jit(solution)/shard_map/ring/ppermute | solution.py:298
  46.8 26.7 %all-to-all-start.1 = ((bf16[32,64,128]{2,1,0:T(8,128)(2,1)}), bf16[32,64,128]{2,1,0:T(8,128)(2,1)S(1)}, u32[]{:S(2)}, u32[]{:S(2)}) async-start(bf16[32,64,128]{2,1,0:T(8,128)(2,1)} %bitcast_bitcast_fusion), calls=%async_computation.1 | async-start | bytes 1048576 | tf_op jit(solution)/shard_map/q_to_heads/all_to_all | solution.py:280
  54.5 3.5 %collective-permute-start.2 = (f32[1,128]{1,0:T(1,128)S(1)}, f32[1,128]{1,0:T(1,128)S(1)}, u32[]{:S(2)}, u32[]{:S(2)}) collective-permute-start(f32[1,128]{1,0:T(1,128)S(1)} %bitcast.39), channel_id=1, source_target_pairs={{0,1},{1,0},{2,3},{3,2},{4,5},{5,4},{6,7},{7,6},{8,9},{9,8},{10,11... | collective-permute-start | bytes 1544 | tf_op jit(solution)/shard_map/key_sums/ppermute | solution.py:295
  58.0 8.6 %collective-permute-start.5 = (f32[1,128]{1,0:T(1,128)S(1)}, f32[1,128]{1,0:T(1,128)S(1)}, u32[]{:S(2)}, u32[]{:S(2)}) collective-permute-start(f32[1,128]{1,0:T(1,128)S(1)} %bitcast_add_fusion), channel_id=1, source_target_pairs={{0,16},{8,24},{16,0},{24,8},{1,17},{9,25},{17,1},{25,9},{2,18},{10... | collective-permute-start | bytes 1544 | tf_op jit(solution)/shard_map/key_sums/ppermute | solution.py:296
  58.0 12.0 %collective-permute-start.4 = (f32[1,128]{1,0:T(1,128)S(1)}, f32[1,128]{1,0:T(1,128)S(1)}, u32[]{:S(2)}, u32[]{:S(2)}) collective-permute-start(f32[1,128]{1,0:T(1,128)S(1)} %bitcast_add_fusion), channel_id=1, source_target_pairs={{0,24},{8,0},{16,8},{24,16},{1,25},{9,1},{17,9},{25,17},{2,26},{10... | collective-permute-start | bytes 1544 | tf_op jit(solution)/shard_map/key_sums/ppermute | solution.py:296
  59.5 13.9 %collective-permute-start.3 = (f32[1,128]{1,0:T(1,128)S(1)}, f32[1,128]{1,0:T(1,128)S(1)}, u32[]{:S(2)}, u32[]{:S(2)}) collective-permute-start(f32[1,128]{1,0:T(1,128)S(1)} %bitcast_add_fusion), channel_id=1, source_target_pairs={{0,8},{8,16},{16,24},{24,0},{1,9},{9,17},{17,25},{25,1},{2,10},{10... | collective-permute-start | bytes 1544 | tf_op jit(solution)/shard_map/key_sums/ppermute | solution.py:296
  66.6 13.4 %collective-permute-start.8 = (bf16[32,2,64,128]{3,2,1,0:T(8,128)(2,1)S(1)}, bf16[32,2,64,128]{3,2,1,0:T(8,128)(2,1)}, u32[]{:S(2)}, u32[]{:S(2)}) collective-permute-start(bf16[32,2,64,128]{3,2,1,0:T(8,128)(2,1)S(1)} %all_to_all.15.o0), channel_id=1, source_target_pairs={{0,1},{1,0},{2,3},{3,2},{4,5},{5,4},{6,7},{7,6},{8,9},{9,8},{10,11... | collective-permute-start | bytes 3145736 | tf_op jit(solution)/shard_map/ring/ppermute | solution.py:300
  73.5 24.7 %copy-start.2 = (bf16[32,2,64,128]{3,2,1,0:T(8,128)(2,1)}, bf16[32,2,64,128]{3,2,1,0:T(8,128)(2,1)S(1)}, u32[]{:S(2)}) copy-start(bf16[32,2,64,128]{3,2,1,0:T(8,128)(2,1)S(1)} %collective-permute-done.1.r0) | copy-start | bytes 3145732
  73.5 6.5 %collective-permute-start.9 = (bf16[32,2,64,128]{3,2,1,0:T(8,128)(2,1)}, bf16[32,2,64,128]{3,2,1,0:T(8,128)(2,1)S(1)}, u32[]{:S(2)}, u32[]{:S(2)}) collective-permute-start(bf16[32,2,64,128]{3,2,1,0:T(8,128)(2,1)} %collective-permute-done.l0), channel_id=1, source_target_pairs={{0,1},{1,0},{2,3},{3,2},{4,5},{5,4},{6,7},{7,6},{8,9},{9,8},{10,11... | collective-permute-start | bytes 3145736 | tf_op jit(solution)/shard_map/ring/ppermute | solution.py:302
  78.2 20.1 %collective-permute-start.12 = (bf16[32,2,64,128]{3,2,1,0:T(8,128)(2,1)S(1)}, bf16[32,2,64,128]{3,2,1,0:T(8,128)(2,1)S(1)}, u32[]{:S(2)}, u32[]{:S(2)}) collective-permute-start(bf16[32,2,64,128]{3,2,1,0:T(8,128)(2,1)S(1)} %collective-permute-done.1.r0), channel_id=1, source_target_pairs={{0,1},{1,0},{2,3},{3,2},{4,5},{5,4},{6,7},{7,6},{8,9},{9,8},{10,11... | collective-permute-start | bytes 3145736 | tf_op jit(solution)/shard_map/ring/ppermute | solution.py:303
  78.5 18.6 %collective-permute-start.7 = (bf16[16,2,64,128]{3,2,1,0:T(8,128)(2,1)S(1)}, bf16[16,2,64,128]{3,2,1,0:T(8,128)(2,1)S(1)}, u32[]{:S(2)}, u32[]{:S(2)}) collective-permute-start(bf16[16,2,64,128]{3,2,1,0:T(8,128)(2,1)S(1)} %slice.26), channel_id=1, source_target_pairs={{0,24},{8,0},{16,8},{24,16},{1,25},{9,1},{17,9},{25,17},{2,26},{10... | collective-permute-start | bytes 1572872 | tf_op jit(solution)/shard_map/ring/ppermute | solution.py:305
  78.5 18.6 %collective-permute-start.6 = (bf16[16,2,64,128]{3,2,1,0:T(8,128)(2,1)S(1)}, bf16[16,2,64,128]{3,2,1,0:T(8,128)(2,1)S(1)}, u32[]{:S(2)}, u32[]{:S(2)}) collective-permute-start(bf16[16,2,64,128]{3,2,1,0:T(8,128)(2,1)S(1)} %slice.25), channel_id=1, source_target_pairs={{0,8},{8,16},{16,24},{24,0},{1,9},{9,17},{17,25},{25,1},{2,10},{10... | collective-permute-start | bytes 1572872 | tf_op jit(solution)/shard_map/ring/ppermute | solution.py:304
  80.0 1.0 copy-start.7
  96.2 1.0 copy-start.4
  97.1 9.1 %collective-permute-start.10 = (bf16[16,2,64,128]{3,2,1,0:T(8,128)(2,1)S(1)}, bf16[16,2,64,128]{3,2,1,0:T(8,128)(2,1)S(1)}, u32[]{:S(2)}, u32[]{:S(2)}) collective-permute-start(bf16[16,2,64,128]{3,2,1,0:T(8,128)(2,1)S(1)} %collective-permute-done.6.a0), channel_id=1, source_target_pairs={{0,1},{1,0},{2,3},{3,2},{4,5},{5,4},{6,7},{7,6},{8,9},{9,8},{10,11... | collective-permute-start | bytes 1572872 | tf_op jit(solution)/shard_map/ring/ppermute | solution.py:317
  97.9 8.3 %collective-permute-start.11 = (bf16[16,2,64,128]{3,2,1,0:T(8,128)(2,1)S(1)}, bf16[16,2,64,128]{3,2,1,0:T(8,128)(2,1)S(1)}, u32[]{:S(2)}, u32[]{:S(2)}) collective-permute-start(bf16[16,2,64,128]{3,2,1,0:T(8,128)(2,1)S(1)} %collective-permute-done.7.b0), channel_id=1, source_target_pairs={{0,1},{1,0},{2,3},{3,2},{4,5},{5,4},{6,7},{7,6},{8,9},{9,8},{10,11... | collective-permute-start | bytes 1572872 | tf_op jit(solution)/shard_map/ring/ppermute | solution.py:318
  98.2 8.0 %copy-start.3 = (bf16[32,2,64,128]{3,2,1,0:T(8,128)(2,1)}, bf16[32,2,64,128]{3,2,1,0:T(8,128)(2,1)S(1)}, u32[]{:S(2)}) copy-start(bf16[32,2,64,128]{3,2,1,0:T(8,128)(2,1)S(1)} %collective-permute-done.12.r1) | copy-start | bytes 3145732
  283.4 22.6 %copy-start.5 = (bf16[64,4096]{1,0:T(8,128)(2,1)S(1)}, bf16[64,4096]{1,0:T(8,128)(2,1)}, u32[]{:S(2)}) copy-start(bf16[64,4096]{1,0:T(8,128)(2,1)} %param.4) | copy-start | bytes 1572868

commit v2 on v1

v2 whole, which is shorter than its diff:
```python
import functools
import math

import jax
import jax.numpy as jnp
from jax import lax
from jax.experimental import pallas as pl
from jax.experimental.pallas import tpu as pltpu
from jax.sharding import Mesh, PartitionSpec as P

HD = 128
SCALE = 1.0 / math.sqrt(HD)
LOG2E = math.log2(math.e)
STEP = 512
VMEM_BYTES = 28 << 20
NZ, NX, NY, NC = 8, 4, 4, 2
T = 64
TOKENS = NZ * NX * NY * NC * T
SRC = NZ * NY
ROWS = SRC * T
TAIL = 16
G = NY * T
LOW, HIGH = 1e-25, 1e25
ALL = ("z", "x", "y", "core")
VMEM = pl.BlockSpec(memory_space=pltpu.VMEM)
ANY = pl.BlockSpec(memory_space=pl.ANY)


def dot_t(a, b):
    return lax.dot_general(a, b, (((1,), (1,)), ((), ())), preferred_element_type=jnp.float32)


def key_mean(q_ref):
    parts = q_ref[:, pl.ds(T, TAIL)].astype(jnp.float32)
    return jnp.sum(jnp.sum(parts, axis=0), axis=0, keepdims=True) / TOKENS


def thirds(value):
    high = value.astype(jnp.bfloat16).astype(jnp.float32)
    mid = (value - high).astype(jnp.bfloat16).astype(jnp.float32)
    return high, mid, value - high - mid


def tail_rows(value, rows):
    which = lax.broadcasted_iota(jnp.int32, (rows, value.shape[1]), 0)
    high, mid, low = (jnp.broadcast_to(v, which.shape) for v in thirds(value))
    picked = jnp.where(which == 1, mid, jnp.where(which == 2, low, 0.0))
    return jnp.where(which == 0, high, picked).astype(jnp.bfloat16)


def side(core):
    return NX - 1 + core * (2 - NX)


def copies(z, srcs, kc, vc, sems):
    out = []
    for s, src in enumerate(srcs):
        part = src.at[pl.ds(z * NY, NY)]
        out.append(pltpu.make_async_copy(part.at[:, 0], kc.at[z, s], sems.at[z]))
        out.append(pltpu.make_async_copy(part.at[:, 1], vc.at[z, s], sems.at[z]))
    return out


def fetch(srcs, kc, vc, sems):
    for z in range(NZ):
        for copy in copies(z, srcs, kc, vc, sems):
            copy.start()


def ready(groups, mean, srcs, kc, vc, sems):
    for z in groups:
        for copy in copies(z, srcs, kc, vc, sems):
            copy.wait()

    @pl.loop(groups[0], groups[-1] + 1)
    def _(z):
        kc[z] = (kc[z].astype(jnp.float32) - mean).astype(jnp.bfloat16)


def attend(q, kc, vc, acc, tot, z, nz, kz, nk, count=None, mask=None):
    count = kc.shape[1] if count is None else count
    keys = nk * count * G
    at = pl.ds(pl.multiple_of(z * G, G), nz * G)
    ks = (pl.ds(kz, nk), pl.ds(0, count))
    rows = q[pl.ds(z * NY, nz * NY), :T].reshape(nz * G, HD)
    k, v = kc[ks].reshape(keys, HD), vc[ks].reshape(keys, HD)
    part, added = None, None
    for i in range(0, keys, STEP):
        p = jnp.exp2(dot_t(rows, k[i : i + STEP]) * (SCALE * LOG2E))
        if mask is not None and i == 0:
            p = jnp.where(mask, p, 0.0)
        for j in range(0, STEP, HD):
            part = p[:, j : j + HD] if part is None else part + p[:, j : j + HD]
        o = jnp.dot(p.astype(jnp.bfloat16), v[i : i + STEP], preferred_element_type=jnp.float32)
        added = o if added is None else added + o
    tot[at] += part
    acc[at] += added


def work(mean, srcs, shift, sems, q, kc, vc, acc, tot, mask=None):
    ns = len(srcs)
    refs = (q, kc, vc, acc, tot)
    ready(range(NZ // 2), mean, srcs, kc, vc, sems)
    big = ns == 4

    @pl.loop(0, 2)
    def _(i):
        if big:
            attend(*refs, 4, 4, i * 2, 2)
        else:
            attend(*refs, 4 + i * 2, 2, 0, 4)

    ready(range(NZ // 2, NZ), mean, srcs, kc, vc, sems)

    @pl.loop(0, 2)
    def _(i):
        attend(*refs, i * 4 + 2, 2, i * 4, 2)

    x = lax.axis_index("x")
    earlier = (x + shift) % NX < x

    @pl.when(earlier)
    def _():
        @pl.loop(0, 2)
        def _(i):
            for j in range(2):
                z = 4 * i + 2 * j
                if mask is None:
                    attend(*refs, z, 2, z, 1)
                else:
                    attend(*refs, z + 1, 1, z, 1)
                    attend(*refs, z, 1, z, 1, ns, mask)
                attend(*refs, z + 1, 1, z + 1, 1, ns, mask)

    @pl.when(jnp.logical_not(earlier))
    def _():
        @pl.loop(0, 2)
        def _(i):
            for j in range(2):
                z = 4 * i + 2 * j
                attend(*refs, z + 1, 1, z, 1)
                if mask is not None:
                    attend(*refs, z, 1, z, 1, 2, mask)
                    attend(*refs, z + 1, 1, z + 1, 1, 2, mask)


def first_kernel(q, o0, o1, m0, m1, acc, tot, kc, vc, sems):
    core = lax.axis_index("core")
    srcs = (o0, o1, m0, m1)
    fetch(srcs, kc, vc, sems)
    acc[...] = jnp.zeros_like(acc)
    tot[...] = jnp.zeros_like(tot)
    shape = (G, 2 * G)
    col = lax.broadcasted_iota(jnp.int32, shape, 1)
    kpos = (col % G) // T * (NC * T) + (core + col // G) % NC * T + col % T
    row = lax.broadcasted_iota(jnp.int32, shape, 0)
    qpos = row // T * (NC * T) + core * T + row % T
    work(key_mean(q), srcs, side(core), sems, q, kc, vc, acc, tot, kpos <= qpos)


def second_kernel(q, s0, s1, acc_in, tot_in, acc, tot, kc, vc, sems, acc0, tot0, sem):
    core = lax.axis_index("core")
    srcs = (s0, s1)
    fetch(srcs, kc, vc, sems)
    state = state_in(acc_in, tot_in, acc0, tot0, sem)
    acc[...] = jnp.zeros_like(acc)
    tot[...] = jnp.zeros_like(tot)
    work(key_mean(q), srcs, side(1 - core), sems, q, kc, vc, acc, tot)
    for copy in state:
        copy.wait()
    acc[...] += acc0[...]
    tot[...] += tot0[...]


def state_in(acc_in, tot_in, acc0, tot0, sem):
    pair = [
        pltpu.make_async_copy(acc_in, acc0, sem.at[0]),
        pltpu.make_async_copy(tot_in, tot0, sem.at[1]),
    ]
    for copy in pair:
        copy.start()
    return pair


def robust(q, srcs, out, acc, run_max, run_sum, stage):
    x, core = lax.axis_index("x"), lax.axis_index("core")
    mean = key_mean(q)
    acc[...] = jnp.zeros_like(acc)
    run_sum[...] = jnp.zeros_like(run_sum)
    run_max[...] = jnp.full_like(run_max, -1e30)
    for s, src in enumerate(srcs):
        kx = (x + (0, side(core), side(1 - core), 2)[s // 2]) % NX
        kcore = (core + s % 2) % NC
        pltpu.sync_copy(src, stage)

        def block(i, carry):
            z, kz = i // NZ, i % NZ

            @pl.when(kz <= z)
            def _():
                at = pl.ds(pl.multiple_of(z * G, G), G)
                part = stage[pl.ds(kz * NY, NY)]
                k = (part[:, 0].reshape(G, HD).astype(jnp.float32) - mean).astype(jnp.bfloat16)
                scores = dot_t(q[pl.ds(z * NY, NY), :T].reshape(G, HD), k) * SCALE
                row = lax.broadcasted_iota(jnp.int32, (G, G), 0)
                col = lax.broadcasted_iota(jnp.int32, (G, G), 1)
                qpos = ((z * NX + x) * NY + row // T) * NC * T + core * T + row % T
                kpos = ((kz * NX + kx) * NY + col // T) * NC * T + kcore * T + col % T
                mask = kpos <= qpos
                old = run_max[at]
                new = jnp.maximum(
                    old, jnp.max(jnp.where(mask, scores, -1e30), axis=1, keepdims=True)
                )
                w = jnp.where(mask, jnp.exp(scores - new[:, :1]), 0.0)
                factor = jnp.exp(old - new)
                run_sum[at] = run_sum[at] * factor + jnp.sum(w, axis=1, keepdims=True)
                acc[at] = acc[at] * factor + jnp.dot(
                    w.astype(jnp.bfloat16),
                    part[:, 1].reshape(G, HD),
                    preferred_element_type=jnp.float32,
                )
                run_max[at] = new

            return carry

        lax.fori_loop(0, NZ * NZ, block, 0)
    out[:, :T] = (acc[...] / run_sum[...]).astype(jnp.bfloat16).reshape(SRC, T, HD)


def far_kernel(
    q, f0, f1, acc_in, tot_in, o0, o1, m0, m1, s0, s1,
    out, acc, tot, kc, vc, sems, acc0, tot0, sem, stage,
):
    far = (f0, f1)
    fetch(far, kc, vc, sems)
    state = state_in(acc_in, tot_in, acc0, tot0, sem)
    acc[...] = jnp.zeros_like(acc)
    tot[...] = jnp.zeros_like(tot)
    work(key_mean(q), far, 2, sems, q, kc, vc, acc, tot)
    for copy in state:
        copy.wait()
    acc[...] += acc0[...]
    tot[...] += tot0[...]
    total = jnp.sum(tot[...], axis=1, keepdims=True)
    out[:, :T] = (acc[...] / total).astype(jnp.bfloat16).reshape(SRC, T, HD)
    tail = tail_rows(key_mean(q), TAIL)
    out[:, T:] = jnp.broadcast_to(tail[None], (SRC, TAIL, HD))
    fine = jnp.where((total > LOW) & (total < HIGH), 0.0, 1.0)

    @pl.when(jnp.max(fine) > 0.0)
    def _():
        robust(q, (o0, o1, m0, m1, s0, s1, f0, f1), out, acc, acc0, tot, stage)


STATE = jax.ShapeDtypeStruct((ROWS, HD), jnp.float32)


def call(kernel, name, ins, outs, scratch, units):
    return functools.partial(
        pl.pallas_call(
            kernel,
            name=name,
            in_specs=ins,
            out_specs=[VMEM] * len(outs),
            out_shape=outs,
            scratch_shapes=scratch,
            compiler_params=pltpu.CompilerParams(vmem_limit_bytes=VMEM_BYTES),
            cost_estimate=pl.CostEstimate(
                flops=units * 32 * G * 2 * G * HD, bytes_accessed=4 << 20, transcendentals=0
            ),
        )
    )


def shards(queries, keys, values):
    def by_head(a):
        return a.reshape(T, SRC, HD).transpose(1, 0, 2)

    def exchange(a):
        return lax.all_to_all(a, ("z", "y"), 0, 0, tiled=True)

    right = [(i, (i + 1) % NX) for i in range(NX)]
    left = [(i, (i - 1) % NX) for i in range(NX)]
    across = [(i, (i + 2) % NX) for i in range(NX)]
    swap = [(0, 1), (1, 0)]
    kv = jnp.stack([by_head(keys), by_head(values)], axis=1)
    with jax.named_scope("kv_to_heads"):
        own = exchange(kv)
    with jax.named_scope("key_sums"):
        sums = jnp.sum(keys.astype(jnp.float32), axis=0).reshape(SRC, HD)
        sums = sums + lax.ppermute(sums, "core", swap)
        sums = sums + sum(lax.ppermute(sums, "x", p) for p in (right, left, across))
        high = lax.reduce_precision(sums, 8, 7)
        mid = lax.reduce_precision(sums - high, 8, 7)
        parts = jnp.stack([high, mid, sums - high - mid], axis=1).astype(jnp.bfloat16)
        parts = jnp.pad(parts, ((0, 0), (0, TAIL - 3), (0, 0)))
    queries, parts, own = lax.optimization_barrier((queries, parts, own))
    with jax.named_scope("q_to_heads"):
        q = exchange(jnp.concatenate([by_head(queries), parts], axis=1))
    ring = [(NC * i, NC * j) for i, j in right] + [(NC * i + 1, NC * j + 1) for i, j in left]
    with jax.named_scope("ring"):
        m0 = lax.ppermute(own, ("x", "core"), ring)
        o1 = lax.ppermute(own, "core", swap)
        m1 = lax.ppermute(o1, ("x", "core"), ring)
        s1 = lax.ppermute(m0, "core", swap)
        s1, q = lax.optimization_barrier((s1, q))
        m0, m1 = lax.optimization_barrier((m0, m1))
        f0 = lax.ppermute(m0, ("x", "core"), ring)
        s0 = lax.ppermute(m1, "core", swap)

    def bufs(ns):
        return [pltpu.VMEM((NZ, ns, NY, T, HD), jnp.bfloat16)] * 2 + [
            pltpu.SemaphoreType.DMA((NZ,))
        ]

    state = [pltpu.VMEM((ROWS, HD), jnp.float32)] * 2
    first = [VMEM] + [ANY] * 4
    acc, tot = call(first_kernel, "first", first, [STATE] * 2, bufs(4), 76)(q, own, o1, m0, m1)
    f0, acc, tot = lax.optimization_barrier((f0, acc, tot))
    with jax.named_scope("ring"):
        f1 = lax.ppermute(f0, "core", swap)
    acc, tot = call(
        second_kernel,
        "second",
        first,
        [STATE] * 2,
        bufs(2) + state + [pltpu.SemaphoreType.DMA((2,))],
        32,
    )(q, s0, s1, acc, tot)
    (out,) = call(
        far_kernel,
        "far",
        [VMEM] + [ANY] * 10,
        [jax.ShapeDtypeStruct((SRC, T + TAIL, HD), jnp.bfloat16)],
        state
        + bufs(2)
        + state
        + [pltpu.SemaphoreType.DMA((2,)), pltpu.VMEM((SRC, 2, T, HD), jnp.bfloat16)],
        32,
    )(q, f0, f1, acc, tot, own, o1, m0, m1, s0, s1)
    with jax.named_scope("home"):
        home = exchange(out)
    attended = home[:, :T].transpose(1, 0, 2).reshape(T, SRC * HD)
    parts = home[:, T : T + 3].astype(jnp.float32)
    mean = (parts[:, 0] + parts[:, 1] + parts[:, 2]).reshape(SRC * HD)
    key_cache = (keys.astype(jnp.float32) - mean).astype(jnp.bfloat16)
    return attended, key_cache


def solution(mesh):
    split = Mesh(mesh.devices.reshape(NZ, NX, NY, NC), ALL)
    spec = P(ALL, None)
    return jax.shard_map(
        shards, mesh=split, in_specs=(spec,) * 3, out_specs=(spec,) * 2, check_vma=False
    )
```

time: 308 us -> 299 us (0.971)
  blocking collectives: 63.8 us -> 20.2 us
  waiting for transfers between devices: 11.4 us -> 34.8 us
  starting transfers between devices: 22.9 us -> 35.8 us
  local copies, waits for them, and re-layouts: 7.2 us -> 2.33 us
    all_to_all x2 -> x1, blocking collectives: 63.8 us -> 20.2 us  [exchange(): return lax.all_to_all(a, ('z', 'y'), 0, 0, tiled=True)]
    all_to_all x1 -> x2, waiting for transfers between devices: 0.01 us -> 16.3 us  [exchange(): return lax.all_to_all(a, ('z', 'y'), 0, 0, tiled=True)]
    ppermute x8 -> x6, waiting for transfers between devices: 0.02 us -> 14.1 us  [the longest x1 9.34 us: shards(): m1 = lax.ppermute(o1, ('x', 'core'), ring)]
    all_to_all x1 -> x2, starting transfers between devices: 7.44 us -> 17.4 us  [exchange(): return lax.all_to_all(a, ('z', 'y'), 0, 0, tiled=True)]
    ppermute x3, waiting for transfers between devices: 10.6 us -> 3.49 us  [shards(): lax.ppermute(sums, 'x', p)]
    pallas_call x1, Pallas kernels: 177 us -> 181 us  [shards(): call(far_kernel, 'far', [VMEM] + [ANY] * 10, [jax.ShapeDtypeStruct((SRC,...]
    ppermute x8 -> x6, starting transfers between devices: 7.9 us -> 10.3 us  [the longest x1 3.41 us: shards(): f0 = lax.ppermute(m0, ('x', 'core'), ring)]
  transfers between devices with their start and end apart: 14 -> 13, of which waited for: 4 -> 6; matrix products, arithmetic and copies ran while one was open for 1% -> 0% of each run, Pallas kernels for 8% -> 7%
where the time goes in v2:
time: 299 us; the launch traced here: 298 us
  Pallas kernels  201 us (67%)
  starting transfers between devices  35.8 us (12%)
  waiting for transfers between devices  34.8 us (12%)
  blocking collectives  20.2 us (7%)
  other arithmetic  3.13 us (1%)
    pallas_call x1, Pallas kernels, shards(): call(far_kernel, 'far', [VMEM] + [ANY] * 10, [jax.ShapeDtypeStruct((SRC,...  181 us
    all_to_all x1, blocking collectives, exchange(): return lax.all_to_all(a, ('z', 'y'), 0, 0, tiled=True)  20.2 us
    all_to_all x2, starting transfers between devices, exchange(): return lax.all_to_all(a, ('z', 'y'), 0, 0, tiled=True)  17.4 us
    all_to_all x2, waiting for transfers between devices, exchange(): return lax.all_to_all(a, ('z', 'y'), 0, 0, tiled=True)  16.3 us
    pallas_call x1, Pallas kernels, shards(): call(first_kernel, 'first', first, [STATE] * 2, bufs(4), 76)  12.9 us
    ppermute x1, waiting for transfers between devices, shards(): m1 = lax.ppermute(o1, ('x', 'core'), ring)  9.34 us
    pallas_call x1, Pallas kernels, shards(): call(second_kernel, 'second', first, [STATE] * 2, bufs(2) + state + [pltp...  7.14 us
  transfers between devices with their start and end apart: 13, of which 6 were waited for; matrix products, arithmetic and copies ran while one was open for 0% of the time, Pallas kernels for 7%

profile of v2, /device:TPU:1, one launch (start us, length us, event | category | flops | bytes accessed | tf_op | source)
XLA Modules:
  0.0 297.8 jit_solution(6972960562693482431)
XLA Ops:
  0.6 0.0 copy-start
  0.6 0.0 copy-start.1
  0.7 1.0 copy-done
  1.7 0.1 bitcast_bitcast_fusion.1
  1.8 0.0 copy-done.1
  1.8 0.1 bitcast_bitcast_fusion.2
  2.0 1.1 pad_maximum_fusion
  3.1 0.0 copy-start.3
  3.1 12.2 %all-to-all-start = ((bf16[32,2,64,128]{3,2,1,0:T(8,128)(2,1)}), bf16[32,2,64,128]{3,2,1,0:T(8,128)(2,1)S(1)}, u32[]{:S(2)}, u32[]{:S(2)}) async-start(bf16[32,2,64,128]{3,2,1,0:T(8,128)(2,1)} %pad_maximum_fusion), calls=%async_computation | async-start | bytes 2097152 | tf_op jit(solution)/shard_map/kv_to_heads/all_to_all | solution.py:280
  15.2 0.1 convert_reduce_fusion
  15.4 1.0 collective-permute-start
  16.4 0.8 collective-permute-done
  17.2 2.7 collective-permute-start.3
  20.0 0.9 collective-permute-start.2
  20.8 0.6 collective-permute-start.1
  21.4 0.0 collective-permute-done.3
  21.5 1.4 collective-permute-done.2
  22.9 2.1 collective-permute-done.1
  25.0 0.1 fusion.5
  25.1 16.3 %all-to-all-done.o0 = bf16[32,2,64,128]{3,2,1,0:T(8,128)(2,1)S(1)} async-done(((bf16[32,2,64,128]{3,2,1,0:T(8,128)(2,1)}), bf16[32,2,64,128]{3,2,1,0:T(8,128)(2,1)S(1)}, u32[]{:S(2)}, u32[]{:S(2)}) %all-to-all-start) | async-done | bytes 1048608 | tf_op jit(solution)/shard_map/kv_to_heads/all_to_all | solution.py:280
  41.5 2.8 collective-permute-start.6
  44.3 2.5 collective-permute-start.4
  46.8 0.0 copy-done.3
  46.8 0.1 bitcast_bitcast_fusion
  46.9 0.9 pad_maximum_fusion.1
  47.8 5.3 %all-to-all-start.1 = ((bf16[32,80,128]{2,1,0:T(8,128)(2,1)}), bf16[32,80,128]{2,1,0:T(8,128)(2,1)S(1)}, u32[]{:S(2)}, u32[]{:S(2)}) async-start(bf16[32,80,128]{2,1,0:T(8,128)(2,1)} %pad_maximum_fusion.1), calls=%async_computation.1 | async-start | bytes 1310720 | tf_op jit(solution)/shard_map/q_to_heads/all_to_all | solution.py:280
  53.1 0.0 collective-permute-done.6.o1
  53.1 0.6 collective-permute-start.7
  53.7 4.8 %collective-permute-done.4.m0 = bf16[32,2,64,128]{3,2,1,0:T(8,128)(2,1)} collective-permute-done((bf16[32,2,64,128]{3,2,1,0:T(8,128)(2,1)S(1)}, bf16[32,2,64,128]{3,2,1,0:T(8,128)(2,1)}, u32[]{:S(2)}, u32[]{:S(2)}) %collective-permute-start.4) | collective-permute-done | bytes 1048608 | tf_op jit(solution)/shard_map/ring/ppermute | solution.py:302
  58.5 1.9 collective-permute-start.5
  60.4 9.3 %collective-permute-done.7.m1 = bf16[32,2,64,128]{3,2,1,0:T(8,128)(2,1)} collective-permute-done((bf16[32,2,64,128]{3,2,1,0:T(8,128)(2,1)S(1)}, bf16[32,2,64,128]{3,2,1,0:T(8,128)(2,1)}, u32[]{:S(2)}, u32[]{:S(2)}) %collective-permute-start.7) | collective-permute-done | bytes 1048608 | tf_op jit(solution)/shard_map/ring/ppermute | solution.py:304
  69.7 3.4 %collective-permute-start.8 = (bf16[32,2,64,128]{3,2,1,0:T(8,128)(2,1)}, bf16[32,2,64,128]{3,2,1,0:T(8,128)(2,1)}, u32[]{:S(2)}, u32[]{:S(2)}) collective-permute-start(bf16[32,2,64,128]{3,2,1,0:T(8,128)(2,1)} %collective-permute-done.4.m0), channel_id=1, source_target_pairs={{0,8},{8,16},{16,24},{24,0},{1,25},{9,1},{17,9},{25,17},{2,10},{10... | collective-permute-start | bytes 3145736 | tf_op jit(solution)/shard_map/ring/ppermute | solution.py:308
  73.2 0.0 collective-permute-start.10
  73.2 0.0 all-to-all-done.1.q
  73.2 0.0 collective-permute-done.5.s1
  73.2 12.9 %first.1 = (f32[2048,128]{1,0:T(8,128)S(1)}, f32[2048,128]{1,0:T(8,128)S(1)}) custom-call(bf16[32,80,128]{2,1,0:T(8,128)(2,1)S(1)} %all-to-all-done.1.q, bf16[32,2,64,128]{3,2,1,0:T(8,128)(2,1)S(1)} %all-to-all-done.o0, bf16[32,2,64,128]{3,2,1,0:T(8,128)(2,1)S(1)} %collective-permute-done.6.o1, bf16[32,2,64,128]{3,2,1,0:T(8,128)(2,1)} %collective-permute-done.4.m0, ...), custom_call_target="tpu_custom_call" | custom-call | flops 40802189312 | bytes 4194304 | tf_op jit(solution)/shard_map/first/pallas_call | solution.py:318
  86.0 0.0 collective-permute-done.8.f0
  86.1 1.9 collective-permute-start.9
  88.0 0.0 collective-permute-done.10.s0
  88.0 7.1 %second.1 = (f32[2048,128]{1,0:T(8,128)S(1)}, f32[2048,128]{1,0:T(8,128)S(1)}) custom-call(bf16[32,80,128]{2,1,0:T(8,128)(2,1)S(1)} %all-to-all-done.1.q, bf16[32,2,64,128]{3,2,1,0:T(8,128)(2,1)} %collective-permute-done.10.s0, bf16[32,2,64,128]{3,2,1,0:T(8,128)(2,1)} %collective-permute-done.5.s1, f32[2048,128]{1,0:T(8,128)S(1)} %get-tuple-element.26.acc_in, ...), custom_call_target="tpu_custom_call" | custom-call | flops 17179869184 | bytes 4194304 | tf_op jit(solution)/shard_map/second/pallas_call | solution.py:322
  95.1 0.0 collective-permute-done.9.f1
  95.1 180.8 %far.1 = bf16[32,80,128]{2,1,0:T(8,128)(2,1)S(1)} custom-call(bf16[32,80,128]{2,1,0:T(8,128)(2,1)S(1)} %all-to-all-done.1.q, bf16[32,2,64,128]{3,2,1,0:T(8,128)(2,1)} %collective-permute-done.8.f0, bf16[32,2,64,128]{3,2,1,0:T(8,128)(2,1)S(1)} %collective-permute-done.9.f1, f32[2048,128]{1,0:T(8,128)S(1)} %get-tuple-element.28.acc_in, ...), custom_call_target="tpu_custom_call" | custom-call | flops 17179869184 | bytes 4194304 | tf_op jit(solution)/shard_map/far/pallas_call | solution.py:330
  275.9 0.0 copy-start.2
  275.9 20.2 %all_to_all.15 = bf16[32,80,128]{2,1,0:T(8,128)(2,1)S(1)} all-to-all(bf16[32,80,128]{2,1,0:T(8,128)(2,1)S(1)} %far.1), channel_id=1, replica_groups=mesh['z'=8,'x'=4,'y'=4,'core'=2] {'z','y'}, dimensions={0} | all-to-all | bytes 1310720 | tf_op jit(solution)/shard_map/home/all_to_all | solution.py:280
  296.1 0.0 copy-done.2
  296.1 0.9 fusion
  297.0 0.8 copy_bitcast_fusion
  (8 shorter events, 0.1 us)
Async XLA Ops:
  0.6 1.0 copy-start
  0.6 1.2 copy-start.1
  3.1 43.7 %copy-start.3 = (bf16[64,4096]{1,0:T(8,128)(2,1)S(1)}, bf16[64,4096]{1,0:T(8,128)(2,1)}, u32[]{:S(2)}) copy-start(bf16[64,4096]{1,0:T(8,128)(2,1)} %param.3) | copy-start | bytes 1572868
  3.1 38.4 %all-to-all-start = ((bf16[32,2,64,128]{3,2,1,0:T(8,128)(2,1)}), bf16[32,2,64,128]{3,2,1,0:T(8,128)(2,1)S(1)}, u32[]{:S(2)}, u32[]{:S(2)}) async-start(bf16[32,2,64,128]{3,2,1,0:T(8,128)(2,1)} %pad_maximum_fusion), calls=%async_computation | async-start | bytes 2097152 | tf_op jit(solution)/shard_map/kv_to_heads/all_to_all | solution.py:280
  15.4 1.9 collective-permute-start
  17.2 4.2 %collective-permute-start.3 = (f32[32,128]{1,0:T(8,128)S(1)}, f32[32,128]{1,0:T(8,128)S(1)}, u32[]{:S(2)}, u32[]{:S(2)}) collective-permute-start(f32[32,128]{1,0:T(8,128)S(1)} %bitcast_add_fusion), channel_id=1, source_target_pairs={{0,16},{8,24},{16,0},{24,8},{1,17},{9,25},{17,1},{25,9},{2,18},{10... | collective-permute-start | bytes 49160 | tf_op jit(solution)/shard_map/key_sums/ppermute | solution.py:292
  20.0 2.9 collective-permute-start.2
  20.8 4.1 %collective-permute-start.1 = (f32[32,128]{1,0:T(8,128)S(1)}, f32[32,128]{1,0:T(8,128)S(1)}, u32[]{:S(2)}, u32[]{:S(2)}) collective-permute-start(f32[32,128]{1,0:T(8,128)S(1)} %bitcast_add_fusion), channel_id=1, source_target_pairs={{0,8},{8,16},{16,24},{24,0},{1,9},{9,17},{17,25},{25,1},{2,10},{10... | collective-permute-start | bytes 49160 | tf_op jit(solution)/shard_map/key_sums/ppermute | solution.py:292
  41.5 11.7 %collective-permute-start.6 = (bf16[32,2,64,128]{3,2,1,0:T(8,128)(2,1)S(1)}, bf16[32,2,64,128]{3,2,1,0:T(8,128)(2,1)S(1)}, u32[]{:S(2)}, u32[]{:S(2)}) collective-permute-start(bf16[32,2,64,128]{3,2,1,0:T(8,128)(2,1)S(1)} %all-to-all-done.o0), channel_id=1, source_target_pairs={{0,1},{1,0},{2,3},{3,2},{4,5},{5,4},{6,7},{7,6},{8,9},{9,8},{10,11... | collective-permute-start | bytes 3145736 | tf_op jit(solution)/shard_map/ring/ppermute | solution.py:303
  44.3 14.2 %collective-permute-start.4 = (bf16[32,2,64,128]{3,2,1,0:T(8,128)(2,1)S(1)}, bf16[32,2,64,128]{3,2,1,0:T(8,128)(2,1)}, u32[]{:S(2)}, u32[]{:S(2)}) collective-permute-start(bf16[32,2,64,128]{3,2,1,0:T(8,128)(2,1)S(1)} %all-to-all-done.o0), channel_id=1, source_target_pairs={{0,8},{8,16},{16,24},{24,0},{1,25},{9,1},{17,9},{25,17},{2,10},{10... | collective-permute-start | bytes 3145736 | tf_op jit(solution)/shard_map/ring/ppermute | solution.py:302
  47.8 25.3 %all-to-all-start.1 = ((bf16[32,80,128]{2,1,0:T(8,128)(2,1)}), bf16[32,80,128]{2,1,0:T(8,128)(2,1)S(1)}, u32[]{:S(2)}, u32[]{:S(2)}) async-start(bf16[32,80,128]{2,1,0:T(8,128)(2,1)} %pad_maximum_fusion.1), calls=%async_computation.1 | async-start | bytes 1310720 | tf_op jit(solution)/shard_map/q_to_heads/all_to_all | solution.py:280
  53.1 16.6 %collective-permute-start.7 = (bf16[32,2,64,128]{3,2,1,0:T(8,128)(2,1)S(1)}, bf16[32,2,64,128]{3,2,1,0:T(8,128)(2,1)}, u32[]{:S(2)}, u32[]{:S(2)}) collective-permute-start(bf16[32,2,64,128]{3,2,1,0:T(8,128)(2,1)S(1)} %collective-permute-done.6.o1), channel_id=1, source_target_pairs={{0,8},{8,16},{16,24},{24,0},{1,25},{9,1},{17,9},{25,17},{2,10},{10... | collective-permute-start | bytes 3145736 | tf_op jit(solution)/shard_map/ring/ppermute | solution.py:304
  58.5 14.7 %collective-permute-start.5 = (bf16[32,2,64,128]{3,2,1,0:T(8,128)(2,1)}, bf16[32,2,64,128]{3,2,1,0:T(8,128)(2,1)}, u32[]{:S(2)}, u32[]{:S(2)}) collective-permute-start(bf16[32,2,64,128]{3,2,1,0:T(8,128)(2,1)} %collective-permute-done.4.m0), channel_id=1, source_target_pairs={{0,1},{1,0},{2,3},{3,2},{4,5},{5,4},{6,7},{7,6},{8,9},{9,8},{10,11... | collective-permute-start | bytes 3145736 | tf_op jit(solution)/shard_map/ring/ppermute | solution.py:305
  69.7 16.3 %collective-permute-start.8 = (bf16[32,2,64,128]{3,2,1,0:T(8,128)(2,1)}, bf16[32,2,64,128]{3,2,1,0:T(8,128)(2,1)}, u32[]{:S(2)}, u32[]{:S(2)}) collective-permute-start(bf16[32,2,64,128]{3,2,1,0:T(8,128)(2,1)} %collective-permute-done.4.m0), channel_id=1, source_target_pairs={{0,8},{8,16},{16,24},{24,0},{1,25},{9,1},{17,9},{25,17},{2,10},{10... | collective-permute-start | bytes 3145736 | tf_op jit(solution)/shard_map/ring/ppermute | solution.py:308
  73.2 14.8 %collective-permute-start.10 = (bf16[32,2,64,128]{3,2,1,0:T(8,128)(2,1)}, bf16[32,2,64,128]{3,2,1,0:T(8,128)(2,1)}, u32[]{:S(2)}, u32[]{:S(2)}) collective-permute-start(bf16[32,2,64,128]{3,2,1,0:T(8,128)(2,1)} %collective-permute-done.7.m1), channel_id=1, source_target_pairs={{0,1},{1,0},{2,3},{3,2},{4,5},{5,4},{6,7},{7,6},{8,9},{9,8},{10,11... | collective-permute-start | bytes 3145736 | tf_op jit(solution)/shard_map/ring/ppermute | solution.py:309
  86.1 9.1 %collective-permute-start.9 = (bf16[32,2,64,128]{3,2,1,0:T(8,128)(2,1)}, bf16[32,2,64,128]{3,2,1,0:T(8,128)(2,1)S(1)}, u32[]{:S(2)}, u32[]{:S(2)}) collective-permute-start(bf16[32,2,64,128]{3,2,1,0:T(8,128)(2,1)} %collective-permute-done.8.f0), channel_id=1, source_target_pairs={{0,1},{1,0},{2,3},{3,2},{4,5},{5,4},{6,7},{7,6},{8,9},{9,8},{10,11... | collective-permute-start | bytes 3145736 | tf_op jit(solution)/shard_map/ring/ppermute | solution.py:321
  275.9 20.2 %copy-start.2 = (bf16[64,4096]{1,0:T(8,128)(2,1)S(1)}, bf16[64,4096]{1,0:T(8,128)(2,1)}, u32[]{:S(2)}) copy-start(bf16[64,4096]{1,0:T(8,128)(2,1)} %param.4) | copy-start | bytes 1572868

commit v3 on v2

--- a/solution.py
+++ b/solution.py
@@ -12,7 +12,7 @@
 SCALE = 1.0 / math.sqrt(HD)
 LOG2E = math.log2(math.e)
 STEP = 512
-VMEM_BYTES = 28 << 20
+VMEM_BYTES = 20 << 20
 NZ, NX, NY, NC = 8, 4, 4, 2
 T = 64
 TOKENS = NZ * NX * NY * NC * T
@@ -67,17 +67,14 @@
             copy.start()
 
 
-def ready(groups, mean, srcs, kc, vc, sems):
-    for z in groups:
-        for copy in copies(z, srcs, kc, vc, sems):
+def ready(first, count, mean, srcs, kc, vc, sems):
+    for i in range(count):
+        for copy in copies(first + i, srcs, kc, vc, sems):
             copy.wait()
-
-    @pl.loop(groups[0], groups[-1] + 1)
-    def _(z):
-        kc[z] = (kc[z].astype(jnp.float32) - mean).astype(jnp.bfloat16)
-
-
-def attend(q, kc, vc, acc, tot, z, nz, kz, nk, count=None, mask=None):
+        kc[first + i] = (kc[first + i].astype(jnp.float32) - mean).astype(jnp.bfloat16)
+
+
+def attend(q, kc, vc, acc, tot, z, nz, kz, nk, count=None, masks=None):
     count = kc.shape[1] if count is None else count
     keys = nk * count * G
     at = pl.ds(pl.multiple_of(z * G, G), nz * G)
@@ -87,8 +84,8 @@
     part, added = None, None
     for i in range(0, keys, STEP):
         p = jnp.exp2(dot_t(rows, k[i : i + STEP]) * (SCALE * LOG2E))
-        if mask is not None and i == 0:
-            p = jnp.where(mask, p, 0.0)
+        if masks is not None:
+            p = jnp.where(masks[i // STEP], p, 0.0)
         for j in range(0, STEP, HD):
             part = p[:, j : j + HD] if part is None else part + p[:, j : j + HD]
         o = jnp.dot(p.astype(jnp.bfloat16), v[i : i + STEP], preferred_element_type=jnp.float32)
@@ -97,56 +94,62 @@
     acc[at] += added
 
 
-def work(mean, srcs, shift, sems, q, kc, vc, acc, tot, mask=None):
+def work(mean, srcs, shifts, sems, q, kc, vc, acc, tot, own=None):
     ns = len(srcs)
     refs = (q, kc, vc, acc, tot)
-    ready(range(NZ // 2), mean, srcs, kc, vc, sems)
-    big = ns == 4
 
     @pl.loop(0, 2)
     def _(i):
-        if big:
-            attend(*refs, 4, 4, i * 2, 2)
-        else:
-            attend(*refs, 4 + i * 2, 2, 0, 4)
-
-    ready(range(NZ // 2, NZ), mean, srcs, kc, vc, sems)
+        ready(i * 2, 2, mean, srcs, kc, vc, sems)
+        attend(*refs, 4, 4, i * 2, 2)
+
+    ready(4, 4, mean, srcs, kc, vc, sems)
 
     @pl.loop(0, 2)
     def _(i):
         attend(*refs, i * 4 + 2, 2, i * 4, 2)
 
     x = lax.axis_index("x")
-    earlier = (x + shift) % NX < x
-
-    @pl.when(earlier)
+    first, second = ((x + shift) % NX < x for shift in shifts)
+    some = jnp.logical_or(first, second)
+
+    def allowed(rows):
+        at = lax.broadcasted_iota(jnp.int32, (rows, 2 * G), 1)
+        ok = jnp.where(at < G, first.astype(jnp.int32), second.astype(jnp.int32))
+        if rows > G:
+            ok = jnp.where(lax.broadcasted_iota(jnp.int32, ok.shape, 0) < G, ok, 1)
+        return ok > 0
+
+    @pl.when(some)
     def _():
         @pl.loop(0, 2)
         def _(i):
+            one = allowed(G)
+            masks = [one] if own is None else [own, one]
             for j in range(2):
                 z = 4 * i + 2 * j
-                if mask is None:
-                    attend(*refs, z, 2, z, 1)
+                if own is None:
+                    attend(*refs, z, 2, z, 1, ns, [allowed(2 * G)])
                 else:
                     attend(*refs, z + 1, 1, z, 1)
-                    attend(*refs, z, 1, z, 1, ns, mask)
-                attend(*refs, z + 1, 1, z + 1, 1, ns, mask)
-
-    @pl.when(jnp.logical_not(earlier))
+                    attend(*refs, z, 1, z, 1, ns, masks)
+                attend(*refs, z + 1, 1, z + 1, 1, ns, masks)
+
+    @pl.when(jnp.logical_not(some))
     def _():
         @pl.loop(0, 2)
         def _(i):
             for j in range(2):
                 z = 4 * i + 2 * j
                 attend(*refs, z + 1, 1, z, 1)
-                if mask is not None:
-                    attend(*refs, z, 1, z, 1, 2, mask)
-                    attend(*refs, z + 1, 1, z + 1, 1, 2, mask)
-
-
-def first_kernel(q, o0, o1, m0, m1, acc, tot, kc, vc, sems):
+                if own is not None:
+                    attend(*refs, z, 1, z, 1, 2, [own])
+                    attend(*refs, z + 1, 1, z + 1, 1, 2, [own])
+
+
+def first_kernel(q, o0, o1, m0, s1, acc, tot, kc, vc, sems):
     core = lax.axis_index("core")
-    srcs = (o0, o1, m0, m1)
+    srcs = (o0, o1, m0, s1)
     fetch(srcs, kc, vc, sems)
     acc[...] = jnp.zeros_like(acc)
     tot[...] = jnp.zeros_like(tot)
@@ -155,17 +158,18 @@
     kpos = (col % G) // T * (NC * T) + (core + col // G) % NC * T + col % T
     row = lax.broadcasted_iota(jnp.int32, shape, 0)
     qpos = row // T * (NC * T) + core * T + row % T
-    work(key_mean(q), srcs, side(core), sems, q, kc, vc, acc, tot, kpos <= qpos)
-
-
-def second_kernel(q, s0, s1, acc_in, tot_in, acc, tot, kc, vc, sems, acc0, tot0, sem):
-    core = lax.axis_index("core")
-    srcs = (s0, s1)
+    shifts = side(core), side(1 - core)
+    work(key_mean(q), srcs, shifts, sems, q, kc, vc, acc, tot, kpos <= qpos)
+
+
+def second_kernel(q, m1, f0, acc_in, tot_in, acc, tot, kc, vc, sems, acc0, tot0, sem):
+    srcs = (m1, f0)
     fetch(srcs, kc, vc, sems)
     state = state_in(acc_in, tot_in, acc0, tot0, sem)
     acc[...] = jnp.zeros_like(acc)
     tot[...] = jnp.zeros_like(tot)
-    work(key_mean(q), srcs, side(1 - core), sems, q, kc, vc, acc, tot)
+    shifts = side(lax.axis_index("core")), 2
+    work(key_mean(q), srcs, shifts, sems, q, kc, vc, acc, tot)
     for copy in state:
         copy.wait()
     acc[...] += acc0[...]
@@ -188,9 +192,9 @@
     acc[...] = jnp.zeros_like(acc)
     run_sum[...] = jnp.zeros_like(run_sum)
     run_max[...] = jnp.full_like(run_max, -1e30)
-    for s, src in enumerate(srcs):
-        kx = (x + (0, side(core), side(1 - core), 2)[s // 2]) % NX
-        kcore = (core + s % 2) % NC
+    for src, shift, other in srcs:
+        kx = (x + shift) % NX
+        kcore = (core + other) % NC
         pltpu.sync_copy(src, stage)
 
         def block(i, carry):
@@ -227,29 +231,33 @@
     out[:, :T] = (acc[...] / run_sum[...]).astype(jnp.bfloat16).reshape(SRC, T, HD)
 
 
-def far_kernel(
-    q, f0, f1, acc_in, tot_in, o0, o1, m0, m1, s0, s1,
+def third_kernel(
+    q, s0, f1, acc_in, tot_in, o0, o1, m0, s1, m1, f0,
     out, acc, tot, kc, vc, sems, acc0, tot0, sem, stage,
 ):
-    far = (f0, f1)
-    fetch(far, kc, vc, sems)
+    core = lax.axis_index("core")
+    last = (s0, f1)
+    fetch(last, kc, vc, sems)
     state = state_in(acc_in, tot_in, acc0, tot0, sem)
     acc[...] = jnp.zeros_like(acc)
     tot[...] = jnp.zeros_like(tot)
-    work(key_mean(q), far, 2, sems, q, kc, vc, acc, tot)
+    work(key_mean(q), last, (side(1 - core), 2), sems, q, kc, vc, acc, tot)
     for copy in state:
         copy.wait()
     acc[...] += acc0[...]
     tot[...] += tot0[...]
     total = jnp.sum(tot[...], axis=1, keepdims=True)
-    out[:, :T] = (acc[...] / total).astype(jnp.bfloat16).reshape(SRC, T, HD)
+    out[:, :T] = (acc[...] * (1.0 / total)).astype(jnp.bfloat16).reshape(SRC, T, HD)
     tail = tail_rows(key_mean(q), TAIL)
     out[:, T:] = jnp.broadcast_to(tail[None], (SRC, TAIL, HD))
     fine = jnp.where((total > LOW) & (total < HIGH), 0.0, 1.0)
 
     @pl.when(jnp.max(fine) > 0.0)
     def _():
-        robust(q, (o0, o1, m0, m1, s0, s1, f0, f1), out, acc, acc0, tot, stage)
+        near, away = side(core), side(1 - core)
+        srcs = [(o0, 0, 0), (o1, 0, 1), (m0, near, 0), (s1, away, 1)]
+        srcs += [(m1, near, 1), (f0, 2, 0), (s0, away, 0), (f1, 2, 1)]
+        robust(q, srcs, out, acc, acc0, tot, stage)
 
 
 STATE = jax.ShapeDtypeStruct((ROWS, HD), jnp.float32)
@@ -304,9 +312,7 @@
         m1 = lax.ppermute(o1, ("x", "core"), ring)
         s1 = lax.ppermute(m0, "core", swap)
         s1, q = lax.optimization_barrier((s1, q))
-        m0, m1 = lax.optimization_barrier((m0, m1))
         f0 = lax.ppermute(m0, ("x", "core"), ring)
-        s0 = lax.ppermute(m1, "core", swap)
 
     def bufs(ns):
         return [pltpu.VMEM((NZ, ns, NY, T, HD), jnp.bfloat16)] * 2 + [
@@ -315,9 +321,10 @@
 
     state = [pltpu.VMEM((ROWS, HD), jnp.float32)] * 2
     first = [VMEM] + [ANY] * 4
-    acc, tot = call(first_kernel, "first", first, [STATE] * 2, bufs(4), 76)(q, own, o1, m0, m1)
-    f0, acc, tot = lax.optimization_barrier((f0, acc, tot))
+    acc, tot = call(first_kernel, "first", first, [STATE] * 2, bufs(4), 76)(q, own, o1, m0, s1)
+    m1, f0, acc, tot = lax.optimization_barrier((m1, f0, acc, tot))
     with jax.named_scope("ring"):
+        s0 = lax.ppermute(m1, "core", swap)
         f1 = lax.ppermute(f0, "core", swap)
     acc, tot = call(
         second_kernel,
@@ -325,19 +332,19 @@
         first,
         [STATE] * 2,
         bufs(2) + state + [pltpu.SemaphoreType.DMA((2,))],
-        32,
-    )(q, s0, s1, acc, tot)
+        36,
+    )(q, m1, f0, acc, tot)
     (out,) = call(
-        far_kernel,
-        "far",
+        third_kernel,
+        "third",
         [VMEM] + [ANY] * 10,
         [jax.ShapeDtypeStruct((SRC, T + TAIL, HD), jnp.bfloat16)],
         state
         + bufs(2)
         + state
         + [pltpu.SemaphoreType.DMA((2,)), pltpu.VMEM((SRC, 2, T, HD), jnp.bfloat16)],
-        32,
-    )(q, f0, f1, acc, tot, own, o1, m0, m1, s0, s1)
+        36,
+    )(q, s0, f1, acc, tot, own, o1, m0, s1, m1, f0)
     with jax.named_scope("home"):
         home = exchange(out)
     attended = home[:, :T].transpose(1, 0, 2).reshape(T, SRC * HD)

time: 299 us -> 295 us (0.987)
    all_to_all x2, waiting for transfers between devices: 16.3 us -> 24.3 us  [exchange(): return lax.all_to_all(a, ('z', 'y'), 0, 0, tiled=True)]
    ppermute x1, waiting for transfers between devices: 9.34 us -> 2.87 us  [shards(): m1 = lax.ppermute(o1, ('x', 'core'), ring)]
  transfers between devices with their start and end apart: 13 -> 13, of which waited for: 6 -> 7; matrix products, arithmetic and copies ran while one was open for 0% -> 0% of each run, Pallas kernels for 7% -> 7%
where the time goes in v3:
time: 295 us
  Pallas kernels  199 us (67%)
  starting transfers between devices  35.9 us (12%)
  waiting for transfers between devices  34.8 us (12%)
  blocking collectives  19 us (6%)
  other arithmetic  3.11 us (1%)
    pallas_call x1, Pallas kernels, shards(): call(third_kernel, 'third', [VMEM] + [ANY] * 10, [jax.ShapeDtypeStruct((S...  179 us
    all_to_all x2, waiting for transfers between devices, exchange(): return lax.all_to_all(a, ('z', 'y'), 0, 0, tiled=True)  24.3 us
    all_to_all x1, blocking collectives, exchange(): return lax.all_to_all(a, ('z', 'y'), 0, 0, tiled=True)  19 us
    all_to_all x2, starting transfers between devices, exchange(): return lax.all_to_all(a, ('z', 'y'), 0, 0, tiled=True)  18.5 us
    pallas_call x1, Pallas kernels, shards(): call(first_kernel, 'first', first, [STATE] * 2, bufs(4), 76)  12.6 us
    pallas_call x1, Pallas kernels, shards(): call(second_kernel, 'second', first, [STATE] * 2, bufs(2) + state + [pltp...  6.94 us
  transfers between devices with their start and end apart: 13, of which 7 were waited for; matrix products, arithmetic and copies ran while one was open for 0% of the time, Pallas kernels for 7%

profile of v3, /device:TPU:1, one launch (start us, length us, event | category | flops | bytes accessed | tf_op | source)
XLA Modules:
  0.0 294.9 jit_solution(4020287327061928985)
XLA Ops:
  0.6 0.0 copy-start
  0.6 0.0 copy-start.1
  0.7 1.0 copy-done
  1.7 0.1 bitcast_bitcast_fusion.1
  1.8 0.0 copy-done.1
  1.8 0.1 bitcast_bitcast_fusion.2
  2.0 1.1 pad_maximum_fusion
  3.1 0.0 copy-start.3
  3.1 12.2 %all-to-all-start = ((bf16[32,2,64,128]{3,2,1,0:T(8,128)(2,1)}), bf16[32,2,64,128]{3,2,1,0:T(8,128)(2,1)S(1)}, u32[]{:S(2)}, u32[]{:S(2)}) async-start(bf16[32,2,64,128]{3,2,1,0:T(8,128)(2,1)} %pad_maximum_fusion), calls=%async_computation | async-start | bytes 2097152 | tf_op jit(solution)/shard_map/kv_to_heads/all_to_all | solution.py:288
  15.2 0.1 convert_reduce_fusion
  15.4 1.0 collective-permute-start
  16.4 0.8 collective-permute-done
  17.2 2.7 collective-permute-start.3
  20.0 0.9 collective-permute-start.2
  20.8 0.6 collective-permute-start.1
  21.4 0.0 collective-permute-done.3
  21.5 1.4 collective-permute-done.2
  22.9 2.1 collective-permute-done.1
  25.0 0.1 fusion.5
  25.1 16.3 %all-to-all-done.o0 = bf16[32,2,64,128]{3,2,1,0:T(8,128)(2,1)S(1)} async-done(((bf16[32,2,64,128]{3,2,1,0:T(8,128)(2,1)}), bf16[32,2,64,128]{3,2,1,0:T(8,128)(2,1)S(1)}, u32[]{:S(2)}, u32[]{:S(2)}) %all-to-all-start) | async-done | bytes 1048608 | tf_op jit(solution)/shard_map/kv_to_heads/all_to_all | solution.py:288
  41.5 2.5 collective-permute-start.4
  43.9 0.0 copy-done.3
  43.9 0.1 bitcast_bitcast_fusion
  44.1 0.9 pad_maximum_fusion.1
  45.0 6.4 %all-to-all-start.1 = ((bf16[32,80,128]{2,1,0:T(8,128)(2,1)}), bf16[32,80,128]{2,1,0:T(8,128)(2,1)S(1)}, u32[]{:S(2)}, u32[]{:S(2)}) async-start(bf16[32,80,128]{2,1,0:T(8,128)(2,1)} %pad_maximum_fusion.1), calls=%async_computation.1 | async-start | bytes 1310720 | tf_op jit(solution)/shard_map/q_to_heads/all_to_all | solution.py:288
  51.3 1.1 collective-permute-start.6
  52.5 3.2 %collective-permute-done.4.m0 = bf16[32,2,64,128]{3,2,1,0:T(8,128)(2,1)S(1)} collective-permute-done((bf16[32,2,64,128]{3,2,1,0:T(8,128)(2,1)S(1)}, bf16[32,2,64,128]{3,2,1,0:T(8,128)(2,1)S(1)}, u32[]{:S(2)}, u32[]{:S(2)}) %collective-permute-start.4) | collective-permute-done | bytes 1048608 | tf_op jit(solution)/shard_map/ring/ppermute | solution.py:310
  55.7 4.6 %collective-permute-start.5 = (bf16[32,2,64,128]{3,2,1,0:T(8,128)(2,1)S(1)}, bf16[32,2,64,128]{3,2,1,0:T(8,128)(2,1)}, u32[]{:S(2)}, u32[]{:S(2)}) collective-permute-start(bf16[32,2,64,128]{3,2,1,0:T(8,128)(2,1)S(1)} %collective-permute-done.4.m0), channel_id=1, source_target_pairs={{0,1},{1,0},{2,3},{3,2},{4,5},{5,4},{6,7},{7,6},{8,9},{9,8},{10,11... | collective-permute-start | bytes 3145736 | tf_op jit(solution)/shard_map/ring/ppermute | solution.py:313
  60.3 1.3 collective-permute-start.8
  61.6 0.0 collective-permute-done.6.o1
  61.6 0.5 collective-permute-start.7
  62.1 8.0 %all-to-all-done.1.q = bf16[32,80,128]{2,1,0:T(8,128)(2,1)S(1)} async-done(((bf16[32,80,128]{2,1,0:T(8,128)(2,1)}), bf16[32,80,128]{2,1,0:T(8,128)(2,1)S(1)}, u32[]{:S(2)}, u32[]{:S(2)}) %all-to-all-start.1) | async-done | bytes 655392 | tf_op jit(solution)/shard_map/q_to_heads/all_to_all | solution.py:288
  70.1 0.0 collective-permute-done.5.s1
  70.1 12.6 %first.1 = (f32[2048,128]{1,0:T(8,128)S(1)}, f32[2048,128]{1,0:T(8,128)S(1)}) custom-call(bf16[32,80,128]{2,1,0:T(8,128)(2,1)S(1)} %all-to-all-done.1.q, bf16[32,2,64,128]{3,2,1,0:T(8,128)(2,1)S(1)} %all-to-all-done.o0, bf16[32,2,64,128]{3,2,1,0:T(8,128)(2,1)} %collective-permute-done.6.o1, bf16[32,2,64,128]{3,2,1,0:T(8,128)(2,1)S(1)} %collective-permute-done.4.m0, ...), custom_call_target="tpu_custom_call" | custom-call | flops 40802189312 | bytes 4194304 | tf_op jit(solution)/shard_map/first/pallas_call | solution.py:324
  82.7 2.9 collective-permute-done.7.m1
  85.6 0.0 collective-permute-done.8.f0
  85.6 2.1 collective-permute-start.9
  87.7 0.0 collective-permute-start.10
  87.7 6.9 %second.1 = (f32[2048,128]{1,0:T(8,128)S(1)}, f32[2048,128]{1,0:T(8,128)S(1)}) custom-call(bf16[32,80,128]{2,1,0:T(8,128)(2,1)S(1)} %all-to-all-done.1.q, bf16[32,2,64,128]{3,2,1,0:T(8,128)(2,1)} %collective-permute-done.7.m1, bf16[32,2,64,128]{3,2,1,0:T(8,128)(2,1)} %collective-permute-done.8.f0, f32[2048,128]{1,0:T(8,128)S(1)} %get-tuple-element.24.acc_in, ...), custom_call_target="tpu_custom_call" | custom-call | flops 19327352832 | bytes 4194304 | tf_op jit(solution)/shard_map/second/pallas_call | solution.py:329
  94.6 0.0 collective-permute-done.9.s0
  94.6 0.0 collective-permute-done.10.f1
  94.6 179.5 %third.1 = bf16[32,80,128]{2,1,0:T(8,128)(2,1)S(1)} custom-call(bf16[32,80,128]{2,1,0:T(8,128)(2,1)S(1)} %all-to-all-done.1.q, bf16[32,2,64,128]{3,2,1,0:T(8,128)(2,1)S(1)} %collective-permute-done.9.s0, bf16[32,2,64,128]{3,2,1,0:T(8,128)(2,1)S(1)} %collective-permute-done.10.f1, f32[2048,128]{1,0:T(8,128)S(1)} %get-tuple-element.26.acc_in, ...), custom_call_target="tpu_custom_call" | custom-call | flops 19327352832 | bytes 4194304 | tf_op jit(solution)/shard_map/third/pallas_call | solution.py:337
  274.1 0.0 copy-start.2
  274.1 19.0 %all_to_all.15 = bf16[32,80,128]{2,1,0:T(8,128)(2,1)S(1)} all-to-all(bf16[32,80,128]{2,1,0:T(8,128)(2,1)S(1)} %third.1), channel_id=1, replica_groups=mesh['z'=8,'x'=4,'y'=4,'core'=2] {'z','y'}, dimensions={0} | all-to-all | bytes 1310720 | tf_op jit(solution)/shard_map/home/all_to_all | solution.py:288
  293.1 0.0 copy-done.2
  293.2 0.9 fusion
  294.0 0.8 copy_bitcast_fusion
  (8 shorter events, 0.1 us)
Async XLA Ops:
  0.6 1.0 copy-start
  0.6 1.2 copy-start.1
  3.1 40.9 %copy-start.3 = (bf16[64,4096]{1,0:T(8,128)(2,1)S(1)}, bf16[64,4096]{1,0:T(8,128)(2,1)}, u32[]{:S(2)}) copy-start(bf16[64,4096]{1,0:T(8,128)(2,1)} %param.3) | copy-start | bytes 1572868
  3.1 38.4 %all-to-all-start = ((bf16[32,2,64,128]{3,2,1,0:T(8,128)(2,1)}), bf16[32,2,64,128]{3,2,1,0:T(8,128)(2,1)S(1)}, u32[]{:S(2)}, u32[]{:S(2)}) async-start(bf16[32,2,64,128]{3,2,1,0:T(8,128)(2,1)} %pad_maximum_fusion), calls=%async_computation | async-start | bytes 2097152 | tf_op jit(solution)/shard_map/kv_to_heads/all_to_all | solution.py:288
  15.4 1.9 collective-permute-start
  17.2 4.2 %collective-permute-start.3 = (f32[32,128]{1,0:T(8,128)S(1)}, f32[32,128]{1,0:T(8,128)S(1)}, u32[]{:S(2)}, u32[]{:S(2)}) collective-permute-start(f32[32,128]{1,0:T(8,128)S(1)} %bitcast_add_fusion), channel_id=1, source_target_pairs={{0,16},{8,24},{16,0},{24,8},{1,17},{9,25},{17,1},{25,9},{2,18},{10... | collective-permute-start | bytes 49160 | tf_op jit(solution)/shard_map/key_sums/ppermute | solution.py:300
  20.0 2.9 collective-permute-start.2
  20.8 4.1 %collective-permute-start.1 = (f32[32,128]{1,0:T(8,128)S(1)}, f32[32,128]{1,0:T(8,128)S(1)}, u32[]{:S(2)}, u32[]{:S(2)}) collective-permute-start(f32[32,128]{1,0:T(8,128)S(1)} %bitcast_add_fusion), channel_id=1, source_target_pairs={{0,8},{8,16},{16,24},{24,0},{1,9},{9,17},{17,25},{25,1},{2,10},{10... | collective-permute-start | bytes 49160 | tf_op jit(solution)/shard_map/key_sums/ppermute | solution.py:300
  41.5 14.2 %collective-permute-start.4 = (bf16[32,2,64,128]{3,2,1,0:T(8,128)(2,1)S(1)}, bf16[32,2,64,128]{3,2,1,0:T(8,128)(2,1)S(1)}, u32[]{:S(2)}, u32[]{:S(2)}) collective-permute-start(bf16[32,2,64,128]{3,2,1,0:T(8,128)(2,1)S(1)} %all-to-all-done.o0), channel_id=1, source_target_pairs={{0,8},{8,16},{16,24},{24,0},{1,25},{9,1},{17,9},{25,17},{2,10},{10... | collective-permute-start | bytes 3145736 | tf_op jit(solution)/shard_map/ring/ppermute | solution.py:310
  45.0 25.1 %all-to-all-start.1 = ((bf16[32,80,128]{2,1,0:T(8,128)(2,1)}), bf16[32,80,128]{2,1,0:T(8,128)(2,1)S(1)}, u32[]{:S(2)}, u32[]{:S(2)}) async-start(bf16[32,80,128]{2,1,0:T(8,128)(2,1)} %pad_maximum_fusion.1), calls=%async_computation.1 | async-start | bytes 1310720 | tf_op jit(solution)/shard_map/q_to_heads/all_to_all | solution.py:288
  51.3 10.2 %collective-permute-start.6 = (bf16[32,2,64,128]{3,2,1,0:T(8,128)(2,1)S(1)}, bf16[32,2,64,128]{3,2,1,0:T(8,128)(2,1)}, u32[]{:S(2)}, u32[]{:S(2)}) collective-permute-start(bf16[32,2,64,128]{3,2,1,0:T(8,128)(2,1)S(1)} %all-to-all-done.o0), channel_id=1, source_target_pairs={{0,1},{1,0},{2,3},{3,2},{4,5},{5,4},{6,7},{7,6},{8,9},{9,8},{10,11... | collective-permute-start | bytes 3145736 | tf_op jit(solution)/shard_map/ring/ppermute | solution.py:311
  55.7 14.4 %collective-permute-start.5 = (bf16[32,2,64,128]{3,2,1,0:T(8,128)(2,1)S(1)}, bf16[32,2,64,128]{3,2,1,0:T(8,128)(2,1)}, u32[]{:S(2)}, u32[]{:S(2)}) collective-permute-start(bf16[32,2,64,128]{3,2,1,0:T(8,128)(2,1)S(1)} %collective-permute-done.4.m0), channel_id=1, source_target_pairs={{0,1},{1,0},{2,3},{3,2},{4,5},{5,4},{6,7},{7,6},{8,9},{9,8},{10,11... | collective-permute-start | bytes 3145736 | tf_op jit(solution)/shard_map/ring/ppermute | solution.py:313
  60.3 25.3 %collective-permute-start.8 = (bf16[32,2,64,128]{3,2,1,0:T(8,128)(2,1)S(1)}, bf16[32,2,64,128]{3,2,1,0:T(8,128)(2,1)}, u32[]{:S(2)}, u32[]{:S(2)}) collective-permute-start(bf16[32,2,64,128]{3,2,1,0:T(8,128)(2,1)S(1)} %collective-permute-done.4.m0), channel_id=1, source_target_pairs={{0,8},{8,16},{16,24},{24,0},{1,25},{9,1},{17,9},{25,17},{2,10},{10... | collective-permute-start | bytes 3145736 | tf_op jit(solution)/shard_map/ring/ppermute | solution.py:315
  61.6 24.0 %collective-permute-start.7 = (bf16[32,2,64,128]{3,2,1,0:T(8,128)(2,1)}, bf16[32,2,64,128]{3,2,1,0:T(8,128)(2,1)}, u32[]{:S(2)}, u32[]{:S(2)}) collective-permute-start(bf16[32,2,64,128]{3,2,1,0:T(8,128)(2,1)} %collective-permute-done.6.o1), channel_id=1, source_target_pairs={{0,8},{8,16},{16,24},{24,0},{1,25},{9,1},{17,9},{25,17},{2,10},{10... | collective-permute-start | bytes 3145736 | tf_op jit(solution)/shard_map/ring/ppermute | solution.py:312
  85.6 9.0 %collective-permute-start.9 = (bf16[32,2,64,128]{3,2,1,0:T(8,128)(2,1)}, bf16[32,2,64,128]{3,2,1,0:T(8,128)(2,1)S(1)}, u32[]{:S(2)}, u32[]{:S(2)}) collective-permute-start(bf16[32,2,64,128]{3,2,1,0:T(8,128)(2,1)} %collective-permute-done.7.m1), channel_id=1, source_target_pairs={{0,1},{1,0},{2,3},{3,2},{4,5},{5,4},{6,7},{7,6},{8,9},{9,8},{10,11... | collective-permute-start | bytes 3145736 | tf_op jit(solution)/shard_map/ring/ppermute | solution.py:327
  87.7 7.0 %collective-permute-start.10 = (bf16[32,2,64,128]{3,2,1,0:T(8,128)(2,1)}, bf16[32,2,64,128]{3,2,1,0:T(8,128)(2,1)S(1)}, u32[]{:S(2)}, u32[]{:S(2)}) collective-permute-start(bf16[32,2,64,128]{3,2,1,0:T(8,128)(2,1)} %collective-permute-done.8.f0), channel_id=1, source_target_pairs={{0,1},{1,0},{2,3},{3,2},{4,5},{5,4},{6,7},{7,6},{8,9},{9,8},{10,11... | collective-permute-start | bytes 3145736 | tf_op jit(solution)/shard_map/ring/ppermute | solution.py:328
  274.1 19.0 %copy-start.2 = (bf16[64,4096]{1,0:T(8,128)(2,1)S(1)}, bf16[64,4096]{1,0:T(8,128)(2,1)}, u32[]{:S(2)}) copy-start(bf16[64,4096]{1,0:T(8,128)(2,1)} %param.4) | copy-start | bytes 1572868

commit v4 on v3

--- a/solution.py
+++ b/solution.py
@@ -11,7 +11,7 @@
 HD = 128
 SCALE = 1.0 / math.sqrt(HD)
 LOG2E = math.log2(math.e)
-STEP = 512
+STEP = 1024
 VMEM_BYTES = 20 << 20
 NZ, NX, NY, NC = 8, 4, 4, 2
 T = 64
@@ -82,13 +82,14 @@
     rows = q[pl.ds(z * NY, nz * NY), :T].reshape(nz * G, HD)
     k, v = kc[ks].reshape(keys, HD), vc[ks].reshape(keys, HD)
     part, added = None, None
-    for i in range(0, keys, STEP):
-        p = jnp.exp2(dot_t(rows, k[i : i + STEP]) * (SCALE * LOG2E))
+    step = min(STEP if masks is None else STEP // 2, keys)
+    for i in range(0, keys, step):
+        p = jnp.exp2(dot_t(rows, k[i : i + step]) * (SCALE * LOG2E))
         if masks is not None:
-            p = jnp.where(masks[i // STEP], p, 0.0)
-        for j in range(0, STEP, HD):
+            p = jnp.where(masks[i // step], p, 0.0)
+        for j in range(0, step, HD):
             part = p[:, j : j + HD] if part is None else part + p[:, j : j + HD]
-        o = jnp.dot(p.astype(jnp.bfloat16), v[i : i + STEP], preferred_element_type=jnp.float32)
+        o = jnp.dot(p.astype(jnp.bfloat16), v[i : i + step], preferred_element_type=jnp.float32)
         added = o if added is None else added + o
     tot[at] += part
     acc[at] += added

time: 295 us -> 295 us (level)
  no operation moved by 1% of the time
where the time goes in v4:
time: 295 us
  Pallas kernels  199 us (67%)
  starting transfers between devices  35.9 us (12%)
  waiting for transfers between devices  35 us (12%)
  blocking collectives  19 us (6%)
  other arithmetic  3.11 us (1%)
    pallas_call x1, Pallas kernels, shards(): call(third_kernel, 'third', [VMEM] + [ANY] * 10, [jax.ShapeDtypeStruct((S...  179 us
    all_to_all x2, waiting for transfers between devices, exchange(): return lax.all_to_all(a, ('z', 'y'), 0, 0, tiled=True)  24.3 us
    all_to_all x1, blocking collectives, exchange(): return lax.all_to_all(a, ('z', 'y'), 0, 0, tiled=True)  19 us
    all_to_all x2, starting transfers between devices, exchange(): return lax.all_to_all(a, ('z', 'y'), 0, 0, tiled=True)  18.5 us
    pallas_call x1, Pallas kernels, shards(): call(first_kernel, 'first', first, [STATE] * 2, bufs(4), 76)  12.3 us
    pallas_call x1, Pallas kernels, shards(): call(second_kernel, 'second', first, [STATE] * 2, bufs(2) + state + [pltp...  6.95 us
  transfers between devices with their start and end apart: 13, of which 7 were waited for; matrix products, arithmetic and copies ran while one was open for 0% of the time, Pallas kernels for 7%

profile of v4, /device:TPU:1, one launch (start us, length us, event | category | flops | bytes accessed | tf_op | source)
XLA Modules:
  0.0 294.8 jit_solution(15018008002738764682)
XLA Ops:
  0.6 0.0 copy-start
  0.6 0.0 copy-start.1
  0.7 1.0 copy-done
  1.7 0.1 bitcast_bitcast_fusion.1
  1.8 0.0 copy-done.1
  1.8 0.1 bitcast_bitcast_fusion.2
  2.0 1.1 pad_maximum_fusion
  3.1 0.0 copy-start.3
  3.1 12.2 %all-to-all-start = ((bf16[32,2,64,128]{3,2,1,0:T(8,128)(2,1)}), bf16[32,2,64,128]{3,2,1,0:T(8,128)(2,1)S(1)}, u32[]{:S(2)}, u32[]{:S(2)}) async-start(bf16[32,2,64,128]{3,2,1,0:T(8,128)(2,1)} %pad_maximum_fusion), calls=%async_computation | async-start | bytes 2097152 | tf_op jit(solution)/shard_map/kv_to_heads/all_to_all | solution.py:289
  15.2 0.1 convert_reduce_fusion
  15.4 1.0 collective-permute-start
  16.4 0.8 collective-permute-done
  17.2 2.7 collective-permute-start.3
  20.0 0.9 collective-permute-start.2
  20.8 0.6 collective-permute-start.1
  21.4 0.0 collective-permute-done.3
  21.5 1.4 collective-permute-done.2
  22.9 2.1 collective-permute-done.1
  25.0 0.1 fusion.5
  25.1 16.3 %all-to-all-done.o0 = bf16[32,2,64,128]{3,2,1,0:T(8,128)(2,1)S(1)} async-done(((bf16[32,2,64,128]{3,2,1,0:T(8,128)(2,1)}), bf16[32,2,64,128]{3,2,1,0:T(8,128)(2,1)S(1)}, u32[]{:S(2)}, u32[]{:S(2)}) %all-to-all-start) | async-done | bytes 1048608 | tf_op jit(solution)/shard_map/kv_to_heads/all_to_all | solution.py:289
  41.5 2.5 collective-permute-start.4
  43.9 0.0 copy-done.3
  43.9 0.1 bitcast_bitcast_fusion
  44.1 0.9 pad_maximum_fusion.1
  45.0 6.4 %all-to-all-start.1 = ((bf16[32,80,128]{2,1,0:T(8,128)(2,1)}), bf16[32,80,128]{2,1,0:T(8,128)(2,1)S(1)}, u32[]{:S(2)}, u32[]{:S(2)}) async-start(bf16[32,80,128]{2,1,0:T(8,128)(2,1)} %pad_maximum_fusion.1), calls=%async_computation.1 | async-start | bytes 1310720 | tf_op jit(solution)/shard_map/q_to_heads/all_to_all | solution.py:289
  51.3 1.1 collective-permute-start.6
  52.5 3.2 %collective-permute-done.4.m0 = bf16[32,2,64,128]{3,2,1,0:T(8,128)(2,1)S(1)} collective-permute-done((bf16[32,2,64,128]{3,2,1,0:T(8,128)(2,1)S(1)}, bf16[32,2,64,128]{3,2,1,0:T(8,128)(2,1)S(1)}, u32[]{:S(2)}, u32[]{:S(2)}) %collective-permute-start.4) | collective-permute-done | bytes 1048608 | tf_op jit(solution)/shard_map/ring/ppermute | solution.py:311
  55.7 4.6 %collective-permute-start.5 = (bf16[32,2,64,128]{3,2,1,0:T(8,128)(2,1)S(1)}, bf16[32,2,64,128]{3,2,1,0:T(8,128)(2,1)}, u32[]{:S(2)}, u32[]{:S(2)}) collective-permute-start(bf16[32,2,64,128]{3,2,1,0:T(8,128)(2,1)S(1)} %collective-permute-done.4.m0), channel_id=1, source_target_pairs={{0,1},{1,0},{2,3},{3,2},{4,5},{5,4},{6,7},{7,6},{8,9},{9,8},{10,11... | collective-permute-start | bytes 3145736 | tf_op jit(solution)/shard_map/ring/ppermute | solution.py:314
  60.3 1.3 collective-permute-start.8
  61.6 0.0 collective-permute-done.6.o1
  61.6 0.5 collective-permute-start.7
  62.1 8.0 %all-to-all-done.1.q = bf16[32,80,128]{2,1,0:T(8,128)(2,1)S(1)} async-done(((bf16[32,80,128]{2,1,0:T(8,128)(2,1)}), bf16[32,80,128]{2,1,0:T(8,128)(2,1)S(1)}, u32[]{:S(2)}, u32[]{:S(2)}) %all-to-all-start.1) | async-done | bytes 655392 | tf_op jit(solution)/shard_map/q_to_heads/all_to_all | solution.py:289
  70.1 0.0 collective-permute-done.5.s1
  70.1 12.3 %first.1 = (f32[2048,128]{1,0:T(8,128)S(1)}, f32[2048,128]{1,0:T(8,128)S(1)}) custom-call(bf16[32,80,128]{2,1,0:T(8,128)(2,1)S(1)} %all-to-all-done.1.q, bf16[32,2,64,128]{3,2,1,0:T(8,128)(2,1)S(1)} %all-to-all-done.o0, bf16[32,2,64,128]{3,2,1,0:T(8,128)(2,1)} %collective-permute-done.6.o1, bf16[32,2,64,128]{3,2,1,0:T(8,128)(2,1)S(1)} %collective-permute-done.4.m0, ...), custom_call_target="tpu_custom_call" | custom-call | flops 40802189312 | bytes 4194304 | tf_op jit(solution)/shard_map/first/pallas_call | solution.py:325
  82.4 3.1 %collective-permute-done.7.m1 = bf16[32,2,64,128]{3,2,1,0:T(8,128)(2,1)} collective-permute-done((bf16[32,2,64,128]{3,2,1,0:T(8,128)(2,1)}, bf16[32,2,64,128]{3,2,1,0:T(8,128)(2,1)}, u32[]{:S(2)}, u32[]{:S(2)}) %collective-permute-start.7) | collective-permute-done | bytes 1048608 | tf_op jit(solution)/shard_map/ring/ppermute | solution.py:313
  85.6 0.0 collective-permute-done.8.f0
  85.6 2.1 collective-permute-start.9
  87.7 0.0 collective-permute-start.10
  87.7 6.9 %second.1 = (f32[2048,128]{1,0:T(8,128)S(1)}, f32[2048,128]{1,0:T(8,128)S(1)}) custom-call(bf16[32,80,128]{2,1,0:T(8,128)(2,1)S(1)} %all-to-all-done.1.q, bf16[32,2,64,128]{3,2,1,0:T(8,128)(2,1)} %collective-permute-done.7.m1, bf16[32,2,64,128]{3,2,1,0:T(8,128)(2,1)} %collective-permute-done.8.f0, f32[2048,128]{1,0:T(8,128)S(1)} %get-tuple-element.24.acc_in, ...), custom_call_target="tpu_custom_call" | custom-call | flops 19327352832 | bytes 4194304 | tf_op jit(solution)/shard_map/second/pallas_call | solution.py:330
  94.6 0.0 collective-permute-done.9.s0
  94.6 0.0 collective-permute-done.10.f1
  94.6 179.4 %third.1 = bf16[32,80,128]{2,1,0:T(8,128)(2,1)S(1)} custom-call(bf16[32,80,128]{2,1,0:T(8,128)(2,1)S(1)} %all-to-all-done.1.q, bf16[32,2,64,128]{3,2,1,0:T(8,128)(2,1)S(1)} %collective-permute-done.9.s0, bf16[32,2,64,128]{3,2,1,0:T(8,128)(2,1)S(1)} %collective-permute-done.10.f1, f32[2048,128]{1,0:T(8,128)S(1)} %get-tuple-element.26.acc_in, ...), custom_call_target="tpu_custom_call" | custom-call | flops 19327352832 | bytes 4194304 | tf_op jit(solution)/shard_map/third/pallas_call | solution.py:338
  274.1 0.0 copy-start.2
  274.1 19.0 %all_to_all.15 = bf16[32,80,128]{2,1,0:T(8,128)(2,1)S(1)} all-to-all(bf16[32,80,128]{2,1,0:T(8,128)(2,1)S(1)} %third.1), channel_id=1, replica_groups=mesh['z'=8,'x'=4,'y'=4,'core'=2] {'z','y'}, dimensions={0} | all-to-all | bytes 1310720 | tf_op jit(solution)/shard_map/home/all_to_all | solution.py:289
  293.1 0.0 copy-done.2
  293.1 0.9 fusion
  294.0 0.8 copy_bitcast_fusion
  (8 shorter events, 0.1 us)
Async XLA Ops:
  0.6 1.0 copy-start
  0.6 1.2 copy-start.1
  3.1 40.9 %copy-start.3 = (bf16[64,4096]{1,0:T(8,128)(2,1)S(1)}, bf16[64,4096]{1,0:T(8,128)(2,1)}, u32[]{:S(2)}) copy-start(bf16[64,4096]{1,0:T(8,128)(2,1)} %param.3) | copy-start | bytes 1572868
  3.1 38.4 %all-to-all-start = ((bf16[32,2,64,128]{3,2,1,0:T(8,128)(2,1)}), bf16[32,2,64,128]{3,2,1,0:T(8,128)(2,1)S(1)}, u32[]{:S(2)}, u32[]{:S(2)}) async-start(bf16[32,2,64,128]{3,2,1,0:T(8,128)(2,1)} %pad_maximum_fusion), calls=%async_computation | async-start | bytes 2097152 | tf_op jit(solution)/shard_map/kv_to_heads/all_to_all | solution.py:289
  15.4 1.9 collective-permute-start
  17.2 4.2 %collective-permute-start.3 = (f32[32,128]{1,0:T(8,128)S(1)}, f32[32,128]{1,0:T(8,128)S(1)}, u32[]{:S(2)}, u32[]{:S(2)}) collective-permute-start(f32[32,128]{1,0:T(8,128)S(1)} %bitcast_add_fusion), channel_id=1, source_target_pairs={{0,16},{8,24},{16,0},{24,8},{1,17},{9,25},{17,1},{25,9},{2,18},{10... | collective-permute-start | bytes 49160 | tf_op jit(solution)/shard_map/key_sums/ppermute | solution.py:301
  20.0 2.9 collective-permute-start.2
  20.8 4.1 %collective-permute-start.1 = (f32[32,128]{1,0:T(8,128)S(1)}, f32[32,128]{1,0:T(8,128)S(1)}, u32[]{:S(2)}, u32[]{:S(2)}) collective-permute-start(f32[32,128]{1,0:T(8,128)S(1)} %bitcast_add_fusion), channel_id=1, source_target_pairs={{0,8},{8,16},{16,24},{24,0},{1,9},{9,17},{17,25},{25,1},{2,10},{10... | collective-permute-start | bytes 49160 | tf_op jit(solution)/shard_map/key_sums/ppermute | solution.py:301
  41.5 14.2 %collective-permute-start.4 = (bf16[32,2,64,128]{3,2,1,0:T(8,128)(2,1)S(1)}, bf16[32,2,64,128]{3,2,1,0:T(8,128)(2,1)S(1)}, u32[]{:S(2)}, u32[]{:S(2)}) collective-permute-start(bf16[32,2,64,128]{3,2,1,0:T(8,128)(2,1)S(1)} %all-to-all-done.o0), channel_id=1, source_target_pairs={{0,8},{8,16},{16,24},{24,0},{1,25},{9,1},{17,9},{25,17},{2,10},{10... | collective-permute-start | bytes 3145736 | tf_op jit(solution)/shard_map/ring/ppermute | solution.py:311
  45.0 25.1 %all-to-all-start.1 = ((bf16[32,80,128]{2,1,0:T(8,128)(2,1)}), bf16[32,80,128]{2,1,0:T(8,128)(2,1)S(1)}, u32[]{:S(2)}, u32[]{:S(2)}) async-start(bf16[32,80,128]{2,1,0:T(8,128)(2,1)} %pad_maximum_fusion.1), calls=%async_computation.1 | async-start | bytes 1310720 | tf_op jit(solution)/shard_map/q_to_heads/all_to_all | solution.py:289
  51.3 10.2 %collective-permute-start.6 = (bf16[32,2,64,128]{3,2,1,0:T(8,128)(2,1)S(1)}, bf16[32,2,64,128]{3,2,1,0:T(8,128)(2,1)}, u32[]{:S(2)}, u32[]{:S(2)}) collective-permute-start(bf16[32,2,64,128]{3,2,1,0:T(8,128)(2,1)S(1)} %all-to-all-done.o0), channel_id=1, source_target_pairs={{0,1},{1,0},{2,3},{3,2},{4,5},{5,4},{6,7},{7,6},{8,9},{9,8},{10,11... | collective-permute-start | bytes 3145736 | tf_op jit(solution)/shard_map/ring/ppermute | solution.py:312
  55.7 14.4 %collective-permute-start.5 = (bf16[32,2,64,128]{3,2,1,0:T(8,128)(2,1)S(1)}, bf16[32,2,64,128]{3,2,1,0:T(8,128)(2,1)}, u32[]{:S(2)}, u32[]{:S(2)}) collective-permute-start(bf16[32,2,64,128]{3,2,1,0:T(8,128)(2,1)S(1)} %collective-permute-done.4.m0), channel_id=1, source_target_pairs={{0,1},{1,0},{2,3},{3,2},{4,5},{5,4},{6,7},{7,6},{8,9},{9,8},{10,11... | collective-permute-start | bytes 3145736 | tf_op jit(solution)/shard_map/ring/ppermute | solution.py:314
  60.3 25.3 %collective-permute-start.8 = (bf16[32,2,64,128]{3,2,1,0:T(8,128)(2,1)S(1)}, bf16[32,2,64,128]{3,2,1,0:T(8,128)(2,1)}, u32[]{:S(2)}, u32[]{:S(2)}) collective-permute-start(bf16[32,2,64,128]{3,2,1,0:T(8,128)(2,1)S(1)} %collective-permute-done.4.m0), channel_id=1, source_target_pairs={{0,8},{8,16},{16,24},{24,0},{1,25},{9,1},{17,9},{25,17},{2,10},{10... | collective-permute-start | bytes 3145736 | tf_op jit(solution)/shard_map/ring/ppermute | solution.py:316
  61.6 24.0 %collective-permute-start.7 = (bf16[32,2,64,128]{3,2,1,0:T(8,128)(2,1)}, bf16[32,2,64,128]{3,2,1,0:T(8,128)(2,1)}, u32[]{:S(2)}, u32[]{:S(2)}) collective-permute-start(bf16[32,2,64,128]{3,2,1,0:T(8,128)(2,1)} %collective-permute-done.6.o1), channel_id=1, source_target_pairs={{0,8},{8,16},{16,24},{24,0},{1,25},{9,1},{17,9},{25,17},{2,10},{10... | collective-permute-start | bytes 3145736 | tf_op jit(solution)/shard_map/ring/ppermute | solution.py:313
  85.6 9.0 %collective-permute-start.9 = (bf16[32,2,64,128]{3,2,1,0:T(8,128)(2,1)}, bf16[32,2,64,128]{3,2,1,0:T(8,128)(2,1)S(1)}, u32[]{:S(2)}, u32[]{:S(2)}) collective-permute-start(bf16[32,2,64,128]{3,2,1,0:T(8,128)(2,1)} %collective-permute-done.7.m1), channel_id=1, source_target_pairs={{0,1},{1,0},{2,3},{3,2},{4,5},{5,4},{6,7},{7,6},{8,9},{9,8},{10,11... | collective-permute-start | bytes 3145736 | tf_op jit(solution)/shard_map/ring/ppermute | solution.py:328
  87.7 7.0 %collective-permute-start.10 = (bf16[32,2,64,128]{3,2,1,0:T(8,128)(2,1)}, bf16[32,2,64,128]{3,2,1,0:T(8,128)(2,1)S(1)}, u32[]{:S(2)}, u32[]{:S(2)}) collective-permute-start(bf16[32,2,64,128]{3,2,1,0:T(8,128)(2,1)} %collective-permute-done.8.f0), channel_id=1, source_target_pairs={{0,1},{1,0},{2,3},{3,2},{4,5},{5,4},{6,7},{7,6},{8,9},{9,8},{10,11... | collective-permute-start | bytes 3145736 | tf_op jit(solution)/shard_map/ring/ppermute | solution.py:329
  274.1 19.0 %copy-start.2 = (bf16[64,4096]{1,0:T(8,128)(2,1)S(1)}, bf16[64,4096]{1,0:T(8,128)(2,1)}, u32[]{:S(2)}) copy-start(bf16[64,4096]{1,0:T(8,128)(2,1)} %param.4) | copy-start | bytes 1572868
